TPU v7x, 512 devices: a whole 4x4x16 slice. The times are simulated.
512 devices in a mesh: expert: 32 (over y, z_lo), dp: 4 (over x), tensor: 4 (over z_hi, core).
Axes of the slice: x: 4, y: 4, z: 16 (z_hi: 2, z_lo: 8; z = z_hi * 8 + z_lo), core: 2. Of those that a mesh axis runs over, the one named last changes fastest.
Arguments:
- tokens: bfloat16 [16384, 1664], P(('expert', 'dp')), may hold values from -6 to 6
- grad_out: bfloat16 [16384, 1664], P(('expert', 'dp')), may hold values from -6 to 6
- picks: int32 [128, 32, 8], P(('expert', 'dp')), may hold values from 0 to 127, as said below
- gates: bfloat16 [128, 32, 8], P(('expert', 'dp')), may hold values from 0.19921875 to 1
- w_in: bfloat16 [32, 1664, 4096], P('expert', 'dp', 'tensor'), may hold values from -0.15625 to 0.15625
- w_out: bfloat16 [32, 4096, 1664], P('expert', 'tensor', 'dp'), may hold values from -0.09375 to 0.09375
- scale_in: float32 [32, 4096], P('expert', 'tensor'), may hold values from 0.012 to 0.06
- scale_out: float32 [32, 1664], P('expert', 'dp'), may hold values from 0.008 to 0.04
Outputs:
- grad_tokens: bfloat16 [16384, 1664], P(('expert', 'dp'), 'tensor')
- grad_gates: float32 [128, 32, 8], P(('expert', 'dp'))
- grad_w_in: bfloat16 [32, 1664, 4096], P('expert', 'dp', 'tensor')
- grad_w_out: bfloat16 [32, 4096, 1664], P('expert', 'tensor', 'dp')
- grad_scale_in: float32 [32, 4096], P('expert', 'tensor')
- grad_scale_out: float32 [32, 1664], P('expert', 'dp')
Inputs may be any that keep to these rules, and one draw needn't show every extreme that they name: `picks`: for each token shard and expert the 8 entries are distinct rows of that shard, counted within its 128 tokens.
All inputs are finite; a program needn't handle non-finite values.
Results may differ from a plain program's by a relative error of at most 0.0075.
Values may be sent and summed in bfloat16 or wider, within the bound.
A program may use at most 64 MiB of HBM per device.

v0:
```python
import jax
import jax.numpy as jnp
from jax import lax
from jax.sharding import PartitionSpec as P

gelu_coeff = 0.7978845608028654
cubic_coeff = 0.044715


def soft_clip(weight, channel_scale):
    scaled = weight.astype(jnp.float32) / channel_scale
    tangent = jnp.tanh(scaled)
    return (channel_scale * tangent, tangent, scaled)


def gelu_parts(hidden):
    inner_arg = gelu_coeff * (hidden + cubic_coeff * hidden * hidden * hidden)
    tangent = jnp.tanh(inner_arg)
    output = 0.5 * hidden * (1.0 + tangent)
    gelu_slope = 0.5 * (1.0 + tangent) + 0.5 * hidden * (1.0 - tangent * tangent) * gelu_coeff * (
        1.0 + 3.0 * cubic_coeff * hidden * hidden
    )
    return (output, gelu_slope)


def local(tokens, grad_out, picks, gates, w_in, w_out, scale_in, scale_out):
    dp_count = lax.axis_size("dp")
    expert_count = lax.axis_size("expert")
    feature_width = tokens.shape[1]
    quant_in, tangent_in, scaled_in = soft_clip(w_in[0], scale_in[0][None, :])
    quant_out, tangent_out, scaled_out = soft_clip(w_out[0], scale_out[0][None, :])
    full_in, full_out = (
        lax.all_gather(quant_in.astype(jnp.bfloat16), "dp", axis=0, tiled=True),
        lax.all_gather(quant_out.astype(jnp.bfloat16), "dp", axis=1, tiled=True),
    )
    chosen = picks[0]
    got_tokens, got_grads, got_gates = (
        lax.all_to_all(tokens[chosen], "expert", split_axis=0, concat_axis=0, tiled=True),
        lax.all_to_all(grad_out[chosen], "expert", split_axis=0, concat_axis=0, tiled=True),
        lax.all_to_all(gates[0], "expert", split_axis=0, concat_axis=0, tiled=True),
    )
    slot_rows = got_tokens.shape[0] * got_tokens.shape[1]
    picked = got_tokens.reshape(slot_rows, feature_width)
    picked_grad = got_grads.reshape(slot_rows, feature_width)
    slot_gates = got_gates.reshape(slot_rows, 1).astype(jnp.float32)
    hidden = jnp.dot(picked, full_in, preferred_element_type=jnp.float32)
    act_value, gelu_slope = gelu_parts(hidden)
    activation = act_value.astype(jnp.bfloat16)
    back_prop = lax.dot_general(
        picked_grad, full_out, (((1,), (1,)), ((), ())), preferred_element_type=jnp.float32
    )
    gate_part = jnp.sum(activation.astype(jnp.float32) * back_prop, axis=1)
    hidden_grad = (slot_gates * back_prop * gelu_slope).astype(jnp.bfloat16)
    out_grad = (slot_gates * picked_grad.astype(jnp.float32)).astype(jnp.bfloat16)
    cols_tokens, cols_grads = (
        lax.all_to_all(picked, "dp", split_axis=1, concat_axis=0, tiled=True),
        lax.all_to_all(out_grad, "dp", split_axis=1, concat_axis=0, tiled=True),
    )
    act_piece = lax.all_gather(activation, "dp", axis=0, tiled=True)
    grad_piece = lax.all_gather(hidden_grad, "dp", axis=0, tiled=True)
    into_in = lax.dot_general(
        cols_tokens, grad_piece, (((0,), (0,)), ((), ())), preferred_element_type=jnp.float32
    )
    into_out = lax.dot_general(
        act_piece, cols_grads, (((0,), (0,)), ((), ())), preferred_element_type=jnp.float32
    )
    total_in = into_in
    total_out = into_out
    factor = (dp_count * slot_rows) ** (-0.5)
    total_in = total_in * factor
    total_out = total_out * factor
    sech_in = 1.0 - tangent_in * tangent_in
    sech_out = 1.0 - tangent_out * tangent_out
    grad_win = (total_in * sech_in).astype(jnp.bfloat16)
    grad_wout = (total_out * sech_out).astype(jnp.bfloat16)
    grad_sin = lax.psum(jnp.sum(total_in * (tangent_in - scaled_in * sech_in), axis=0), "dp")
    grad_sout = lax.psum(
        jnp.sum(total_out * (tangent_out - scaled_out * sech_out), axis=0), "tensor"
    )
    token_grad = lax.dot_general(
        hidden_grad, full_in, (((1,), (1,)), ((), ())), preferred_element_type=jnp.float32
    )
    flat_chosen = chosen.reshape(-1)
    back_rows, back_gates = (
        lax.all_to_all(
            token_grad.reshape(expert_count, -1, feature_width),
            "expert",
            split_axis=0,
            concat_axis=0,
            tiled=True,
        ),
        lax.all_to_all(
            gate_part.reshape(expert_count, -1), "expert", split_axis=0, concat_axis=0, tiled=True
        ),
    )
    partial_rows = jax.ops.segment_sum(
        back_rows.reshape(-1, feature_width), flat_chosen, num_segments=tokens.shape[0]
    )
    summed = lax.psum_scatter(partial_rows, "tensor", scatter_dimension=1, tiled=True)
    grad_gates = lax.psum(back_gates, "tensor")
    return (
        summed.astype(jnp.bfloat16),
        grad_gates[None],
        grad_win[None],
        grad_wout[None],
        grad_sin[None],
        grad_sout[None],
    )


def solution(mesh):
    placed = (
        P(("expert", "dp"), None),
        P(("expert", "dp"), None),
        P(("expert", "dp"), None, None),
        P(("expert", "dp"), None, None),
        P("expert", "dp", "tensor"),
        P("expert", "tensor", "dp"),
        P("expert", "tensor"),
        P("expert", "dp"),
    )
    return jax.shard_map(
        local,
        mesh=mesh,
        in_specs=placed,
        out_specs=(
            P(("expert", "dp"), "tensor"),
            P(("expert", "dp"), None, None),
            P("expert", "dp", "tensor"),
            P("expert", "tensor", "dp"),
            P("expert", "tensor"),
            P("expert", "dp"),
        ),
        check_vma=False,
    )
```

profile of v0, /device:TPU:1, one launch (start us, length us, event | category | flops | bytes accessed | tf_op | source)
XLA Modules:
  0.0 337.2 jit_solution(7227023895264988572)
XLA Ops:
  10.4 16.1 %all-to-all-start = ((bf16[32,1,8]{2,1,0:T(2,128)(2,1)}), bf16[32,1,8]{2,1,0:T(2,128)(2,1)S(1)}, u32[]{:S(2)}, u32[]{:S(2)}) async-start(bf16[32,1,8]{2,1,0:T(2,128)(2,1)} %copy.33), calls=%async_computation | async-start | bytes 32768 | tf_op jit(solution)/shard_map/all_to_all | solution.py:40
  28.9 8.8 %all-to-all-done = bf16[32,1,8]{2,1,0:T(2,128)(2,1)S(1)} async-done(((bf16[32,1,8]{2,1,0:T(2,128)(2,1)}), bf16[32,1,8]{2,1,0:T(2,128)(2,1)S(1)}, u32[]{:S(2)}, u32[]{:S(2)}) %all-to-all-start) | async-done | bytes 544 | tf_op jit(solution)/shard_map/all_to_all | solution.py:40
  37.7 3.9 %all-to-all-start.1 = ((bf16[32,8,1664]{2,1,0:T(8,128)(2,1)}), bf16[32,8,1664]{2,1,0:T(8,128)(2,1)S(1)}, u32[]{:S(2)}, u32[]{:S(2)}) async-start(bf16[32,8,1664]{2,1,0:T(8,128)(2,1)} %bitcast.2), calls=%async_computation.1 | async-start | bytes 1703936 | tf_op jit(solution)/shard_map/all_to_all | solution.py:39
  45.3 38.8 %all-to-all-done.1 = bf16[32,8,1664]{2,1,0:T(8,128)(2,1)S(1)} async-done(((bf16[32,8,1664]{2,1,0:T(8,128)(2,1)}), bf16[32,8,1664]{2,1,0:T(8,128)(2,1)S(1)}, u32[]{:S(2)}, u32[]{:S(2)}) %all-to-all-start.1) | async-done | bytes 852000 | tf_op jit(solution)/shard_map/all_to_all | solution.py:39
  85.0 5.4 %all-to-all-start.2 = ((bf16[32,8,1664]{2,1,0:T(8,128)(2,1)}), bf16[32,8,1664]{2,1,0:T(8,128)(2,1)S(1)}, u32[]{:S(2)}, u32[]{:S(2)}) async-start(bf16[32,8,1664]{2,1,0:T(8,128)(2,1)} %bitcast.6), calls=%async_computation.2 | async-start | bytes 1703936 | tf_op jit(solution)/shard_map/all_to_all | solution.py:38
  90.6 3.5 %reshape.97 = f32[256,4,416]{2,1,0:T(4,128)S(1)} reshape(bf16[32,8,1664]{2,1,0:T(8,128)(2,1)} %copy-done.5) | data formatting | bytes 2555904 | tf_op jit(solution)/shard_map/convert_element_type | solution.py:54
  95.6 2.6 copy.38
  98.2 34.7 %all-to-all-done.2 = bf16[32,8,1664]{2,1,0:T(8,128)(2,1)S(1)} async-done(((bf16[32,8,1664]{2,1,0:T(8,128)(2,1)}), bf16[32,8,1664]{2,1,0:T(8,128)(2,1)S(1)}, u32[]{:S(2)}, u32[]{:S(2)}) %all-to-all-start.2) | async-done | bytes 852000 | tf_op jit(solution)/shard_map/all_to_all | solution.py:38
  133.0 4.0 %all-to-all-start.6 = ((bf16[256,4,416]{0,2,1:T(8,128)(2,1)}), bf16[256,4,416]{0,2,1:T(8,128)(2,1)S(1)}, u32[]{:S(2)}, u32[]{:S(2)}) async-start(bf16[256,4,416]{0,2,1:T(8,128)(2,1)} %copy.38), calls=%async_computation.6 | async-start | bytes 1703936 | tf_op jit(solution)/shard_map/all_to_all | solution.py:57
  137.0 4.1 %fusion.11 = f32[256,1024]{1,0:T(8,128)} fusion(bf16[1664,1024]{1,0:T(8,128)(2,1)} %all-gather.7.cloned.1.call-done, bf16[32,8,1664]{2,1,0:T(8,128)(2,1)S(1)} %all-to-all-done.2), kind=kOutput, calls=%fused_computation.30 | convolution fusion | flops 872415232 | bytes 5308416 | tf_op jit(solution)/shard_map/dot_general | solution.py:46
  141.1 4.7 %multiply_reduce_fusion.2 = (f32[256]{0:T(256)S(1)}, bf16[256,1024]{1,0:T(8,128)(2,1)}, bf16[256,1024]{1,0:T(8,128)(2,1)S(1)}) fusion(f32[256,1024]{1,0:T(8,128)} %fusion.11, f32[256]{0:T(256)S(1)} %reshape.94, bf16[1024,1664]{0,1:T(8,128)(2,1)} %all-gather.5.cloned.1.call-done, bf16[32,8,1664]{2,1,0:T(8,128)(2,1)S(1)} %copy-done.6), kind=kOutput, calls=%fused_computation.26 | convolution fusion | flops 878968576 | bytes 6359040 | tf_op jit(solution)/shard_map/dot_general | solution.py:49
  145.9 4.5 %convolution_bitcast_fusion = f32[32,8,1664]{2,1,0:T(8,128)} fusion(bf16[256,1024]{1,0:T(8,128)(2,1)S(1)} %get-tuple-element.32, bf16[1664,1024]{1,0:T(8,128)(2,1)} %all-gather.7.cloned.1.call-done), kind=kOutput, calls=%fused_computation.3 | convolution fusion | flops 872415232 | bytes 5636096 | tf_op jit(solution)/shard_map/dot_general | solution.py:80
  151.3 5.5 %all-to-all-start.3 = ((f32[32,8,1664]{2,1,0:T(8,128)}), f32[32,8,1664]{2,1,0:T(8,128)S(1)}, u32[]{:S(2)}, u32[]{:S(2)}) async-start(f32[32,8,1664]{2,1,0:T(8,128)} %convolution_bitcast_fusion), calls=%async_computation.3 | async-start | bytes 3407872 | tf_op jit(solution)/shard_map/all_to_all | solution.py:85
  158.1 3.5 %all_to_all.57 = bf16[256,4,416]{2,1,0:T(4,128)(2,1)S(1)} reshape(bf16[32,8,1664]{2,1,0:T(8,128)(2,1)} %copy-done.4) | data formatting | bytes 1703936 | tf_op jit(solution)/shard_map/all_to_all | solution.py:56
  163.3 70.2 %all-to-all-done.3 = f32[32,8,1664]{2,1,0:T(8,128)S(1)} async-done(((f32[32,8,1664]{2,1,0:T(8,128)}), f32[32,8,1664]{2,1,0:T(8,128)S(1)}, u32[]{:S(2)}, u32[]{:S(2)}) %all-to-all-start.3) | async-done | bytes 1703968 | tf_op jit(solution)/shard_map/all_to_all | solution.py:85
  233.5 4.2 %all-to-all-start.5 = ((bf16[256,4,416]{0,2,1:T(8,128)(2,1)}), bf16[256,4,416]{0,2,1:T(8,128)(2,1)S(1)}, u32[]{:S(2)}, u32[]{:S(2)}) async-start(bf16[256,4,416]{0,2,1:T(8,128)(2,1)} %copy.36), calls=%async_computation.5 | async-start | bytes 1703936 | tf_op jit(solution)/shard_map/all_to_all | solution.py:56
  237.9 4.4 %scatter_custom_fusion = f32[128,1664]{1,0:T(8,128)} fusion(s32[256]{0:T(256)S(1)} %reshape.116, f32[32,8,1664]{2,1,0:T(8,128)S(1)} %all-to-all-done.3, f32[]{:T(128)} %constant.9.clone.1), kind=kCustom, calls=%fused_computation.7 | custom fusion | flops 425984 | bytes 2555908 | tf_op jit(solution)/shard_map/scatter-add | solution.py:96
  245.8 2.6 all-to-all-done.5
  250.1 12.2 %all-to-all-start.4 = ((f32[32,1,8]{2,1,0:T(1,128)}), f32[32,1,8]{2,1,0:T(1,128)S(1)}, u32[]{:S(2)}, u32[]{:S(2)}) async-start(f32[32,1,8]{2,1,0:T(1,128)} %bitcast.12), calls=%async_computation.4 | async-start | bytes 32768 | tf_op jit(solution)/shard_map/all_to_all | solution.py:92
  262.4 4.4 %fusion.10 = (bf16[1,1024,416]{1,2,0:T(8,128)(2,1)}, f32[416]{0:T(512)S(1)}) fusion(f32[416]{0:T(512)S(1)} %bitcast.75, bf16[1,1024,416]{1,2,0:T(8,128)(2,1)S(1)} %copy-done.8, bf16[1024,416]{0,1:T(8,128)(2,1)} %bitcast.68, bf16[1024,1024]{1,0:T(8,128)(2,1)} %all-gather.11.cloned.1.call-done), kind=kOutput, calls=%fused_computation.29 | convolution fusion | flops 877100672 | bytes 4656384 | tf_op jit(solution)/shard_map/dot_general | solution.py:64
  266.8 6.8 %all-to-all-done.4 = f32[32,1,8]{2,1,0:T(1,128)S(1)} async-done(((f32[32,1,8]{2,1,0:T(1,128)}), f32[32,1,8]{2,1,0:T(1,128)S(1)}, u32[]{:S(2)}, u32[]{:S(2)}) %all-to-all-start.4) | async-done | bytes 1056 | tf_op jit(solution)/shard_map/all_to_all | solution.py:92
  273.6 41.7 %all-reduce = (f32[1,32,8]{2,1,0:T(8,128)S(1)}, f32[1,416]{1,0:T(1,128)}) all-reduce(f32[1,32,8]{2,1,0:T(8,128)S(1)} %bitcast.70, f32[1,416]{1,0:T(1,128)S(1)} %bitcast.77), channel_id=1, replica_groups=mesh['expert'=32,'dp'=4,'tensor'=4] {'tensor'}, use_global_device_ids=true, to_apply=%region_3.0 | all-reduce | flops 672 | bytes 5376 | tf_op jit(solution)/shard_map/psum | solution.py:100
  315.9 3.9 %multiply_reduce_fusion.1 = (f32[1024]{0:T(1024)S(1)}, bf16[1,416,1024]{2,1,0:T(8,128)(2,1)}) fusion(f32[1024]{0:T(1024)S(1)} %bitcast.72, bf16[1,416,1024]{2,1,0:T(8,128)(2,1)S(1)} %copy-done.9, bf16[1024,416]{0,1:T(8,128)(2,1)S(1)} %bitcast.67, bf16[1024,1024]{1,0:T(8,128)(2,1)} %all-gather.9.cloned.1.call-done), kind=kOutput, calls=%fused_computation.10 | convolution fusion | flops 877100032 | bytes 4661248 | tf_op jit(solution)/shard_map/dot_general | solution.py:61
  319.9 9.0 %psum.22 = f32[1,1024]{1,0:T(1,128)} all-reduce(f32[1,1024]{1,0:T(1,128)S(1)} %bitcast.73), channel_id=1, replica_groups=mesh['expert'=32,'dp'=4,'tensor'=4] {'dp'}, use_global_device_ids=true, to_apply=%region_5.0 | all-reduce | flops 1024 | bytes 8192 | tf_op jit(solution)/shard_map/psum | solution.py:76
  (70 shorter events, 23.4 us)
Async XLA Ops:
  7.2 19.5 %copy-start = (bf16[128,1664]{1,0:T(8,128)(2,1)S(1)}, bf16[128,1664]{1,0:T(8,128)(2,1)}, u32[]{:S(2)}) copy-start(bf16[128,1664]{1,0:T(8,128)(2,1)} %param.9) | copy-start | bytes 1277956
  7.2 2.5 copy-start.15
  7.2 19.3 %copy-start.12 = (s32[1,32,8]{1,2,0:T(8,128)S(1)}, s32[1,32,8]{1,2,0:T(8,128)}, u32[]{:S(2)}) copy-start(s32[1,32,8]{1,2,0:T(8,128)} %param.10) | copy-start | bytes 3076
  7.2 129.8 %all-gather.7.cloned.1.call-start = ((), (), s32[]{:S(2)}) async-start(), calls=%async_computation.9 | async-start | bytes 4259840 | tf_op jit(solution)/shard_map/all_gather | solution.py:33
  10.4 27.4 %all-to-all-start = ((bf16[32,1,8]{2,1,0:T(2,128)(2,1)}), bf16[32,1,8]{2,1,0:T(2,128)(2,1)S(1)}, u32[]{:S(2)}, u32[]{:S(2)}) async-start(bf16[32,1,8]{2,1,0:T(2,128)(2,1)} %copy.33), calls=%async_computation | async-start | bytes 32768 | tf_op jit(solution)/shard_map/all_to_all | solution.py:40
  28.9 12.8 %copy-start.7 = (bf16[1,1024,416]{1,2,0:T(8,128)(2,1)S(1)}, bf16[1,1024,416]{1,2,0:T(8,128)(2,1)}, u32[]{:S(2)}) copy-start(bf16[1,1024,416]{1,2,0:T(8,128)(2,1)} %param.13) | copy-start | bytes 2555908
  28.9 12.8 %copy-start.14 = (f32[1,416]{1,0:T(1,128)S(1)}, f32[1,416]{1,0:T(1,128)}, u32[]{:S(2)}) copy-start(f32[1,416]{1,0:T(1,128)} %param.15) | copy-start | bytes 4996
  37.7 46.4 %all-to-all-start.1 = ((bf16[32,8,1664]{2,1,0:T(8,128)(2,1)}), bf16[32,8,1664]{2,1,0:T(8,128)(2,1)S(1)}, u32[]{:S(2)}, u32[]{:S(2)}) async-start(bf16[32,8,1664]{2,1,0:T(8,128)(2,1)} %bitcast.2), calls=%async_computation.1 | async-start | bytes 1703936 | tf_op jit(solution)/shard_map/all_to_all | solution.py:39
  41.7 99.5 %all-gather.5.cloned.1.call-start = ((), (), s32[]{:S(2)}) async-start(), calls=%async_computation.8 | async-start | bytes 4259840 | tf_op jit(solution)/shard_map/all_gather | solution.py:34
  85.0 47.9 %all-to-all-start.2 = ((bf16[32,8,1664]{2,1,0:T(8,128)(2,1)}), bf16[32,8,1664]{2,1,0:T(8,128)(2,1)S(1)}, u32[]{:S(2)}, u32[]{:S(2)}) async-start(bf16[32,8,1664]{2,1,0:T(8,128)(2,1)} %bitcast.6), calls=%async_computation.2 | async-start | bytes 1703936 | tf_op jit(solution)/shard_map/all_to_all | solution.py:38
  133.0 8.2 %copy-start.4 = (bf16[32,8,1664]{2,1,0:T(8,128)(2,1)}, bf16[32,8,1664]{2,1,0:T(8,128)(2,1)S(1)}, u32[]{:S(2)}) copy-start(bf16[32,8,1664]{2,1,0:T(8,128)(2,1)S(1)} %all-to-all-done.2) | copy-start | bytes 2555908
  133.0 17.4 %all-to-all-start.6 = ((bf16[256,4,416]{0,2,1:T(8,128)(2,1)}), bf16[256,4,416]{0,2,1:T(8,128)(2,1)S(1)}, u32[]{:S(2)}, u32[]{:S(2)}) async-start(bf16[256,4,416]{0,2,1:T(8,128)(2,1)} %copy.38), calls=%async_computation.6 | async-start | bytes 1703936 | tf_op jit(solution)/shard_map/all_to_all | solution.py:57
  137.0 4.1 %copy-start.6 = (bf16[32,8,1664]{2,1,0:T(8,128)(2,1)S(1)}, bf16[32,8,1664]{2,1,0:T(8,128)(2,1)}, u32[]{:S(2)}) copy-start(bf16[32,8,1664]{2,1,0:T(8,128)(2,1)} %copy-done.5) | copy-start | bytes 2555908
  145.9 4.5 %copy-start.11 = (bf16[256,1024]{1,0:T(8,128)(2,1)}, bf16[256,1024]{1,0:T(8,128)(2,1)S(1)}, u32[]{:S(2)}) copy-start(bf16[256,1024]{1,0:T(8,128)(2,1)S(1)} %get-tuple-element.32) | copy-start | bytes 1572868
  151.3 82.2 %all-to-all-start.3 = ((f32[32,8,1664]{2,1,0:T(8,128)}), f32[32,8,1664]{2,1,0:T(8,128)S(1)}, u32[]{:S(2)}, u32[]{:S(2)}) async-start(f32[32,8,1664]{2,1,0:T(8,128)} %convolution_bitcast_fusion), calls=%async_computation.3 | async-start | bytes 3407872 | tf_op jit(solution)/shard_map/all_to_all | solution.py:85
  156.8 105.6 %all-gather.11.cloned.1.call-start = ((), (), s32[]{:S(2)}) async-start(), calls=%async_computation.11 | async-start | bytes 2621440 | tf_op jit(solution)/shard_map/all_gather | solution.py:59
  157.5 158.4 %all-gather.9.cloned.1.call-start = ((), (), s32[]{:S(2)}) async-start(), calls=%async_computation.10 | async-start | bytes 2621440 | tf_op jit(solution)/shard_map/all_gather | solution.py:60
  233.5 14.9 %all-to-all-start.5 = ((bf16[256,4,416]{0,2,1:T(8,128)(2,1)}), bf16[256,4,416]{0,2,1:T(8,128)(2,1)S(1)}, u32[]{:S(2)}, u32[]{:S(2)}) async-start(bf16[256,4,416]{0,2,1:T(8,128)(2,1)} %copy.36), calls=%async_computation.5 | async-start | bytes 1703936 | tf_op jit(solution)/shard_map/all_to_all | solution.py:56
  237.7 91.2 %reduce-scatter.4.cloned.1.call-start = ((), (), s32[]{:S(2)}) async-start(), calls=%async_computation.12 | async-start | bytes 1064960
  244.8 17.6 %copy-start.8 = (bf16[1,1024,416]{1,2,0:T(8,128)(2,1)S(1)}, bf16[1,1024,416]{1,2,0:T(8,128)(2,1)}, u32[]{:S(2)}) copy-start(bf16[1,1024,416]{1,2,0:T(8,128)(2,1)} %param.13) | copy-start | bytes 2555908
  250.1 23.4 %all-to-all-start.4 = ((f32[32,1,8]{2,1,0:T(1,128)}), f32[32,1,8]{2,1,0:T(1,128)S(1)}, u32[]{:S(2)}, u32[]{:S(2)}) async-start(f32[32,1,8]{2,1,0:T(1,128)} %bitcast.12), calls=%async_computation.4 | async-start | bytes 32768 | tf_op jit(solution)/shard_map/all_to_all | solution.py:92
  262.4 53.6 %copy-start.9 = (bf16[1,416,1024]{2,1,0:T(8,128)(2,1)S(1)}, bf16[1,416,1024]{2,1,0:T(8,128)(2,1)}, u32[]{:S(2)}) copy-start(bf16[1,416,1024]{2,1,0:T(8,128)(2,1)} %param.12) | copy-start | bytes 2555908
  262.4 53.5 %copy-start.10 = (bf16[4,52,8,256]{3,2,0,1:T(8,128)(2,1)S(1)}, bf16[4,52,8,256]{3,2,0,1:T(8,128)(2,1)}, u32[]{:S(2)}) copy-start(bf16[4,52,8,256]{3,2,0,1:T(8,128)(2,1)} %copy.44) | copy-start | bytes 2555908
  262.4 53.5 %copy-start.13 = (f32[1,1024]{1,0:T(1,128)S(1)}, f32[1,1024]{1,0:T(1,128)}, u32[]{:S(2)}) copy-start(f32[1,1024]{1,0:T(1,128)} %param.14) | copy-start | bytes 12292
  (4 other events, 5.7 us)
Sparse Core Ops, SparseCore 0:
  10.7 54.6 all-gather.6
  67.5 49.6 all-gather.4
  159.7 39.5 all-gather.10
  201.2 38.5 all-gather.8
  244.9 70.9 reduce-scatter.3
where the time goes:
time: 339 us; the launch traced here: 337 us
  waiting for transfers between devices  163 us (48%)
  starting transfers between devices  51.7 us (15%)
  blocking collectives  50.7 us (15%)
  local copies, waits for them, and re-layouts  26.5 us (8%)
  matrix products  21.7 us (6%)
  between operations  14 us (4%)
  other arithmetic  9.61 us (3%)
    all_to_all x1, waiting for transfers between devices, local(): lax.all_to_all(token_grad.reshape(expert_count, -1, feature_width), 'expe...  70.2 us
    psum x1, blocking collectives, local(): grad_gates = lax.psum(back_gates, 'tensor')  41.7 us
    all_to_all x1, waiting for transfers between devices, local(): lax.all_to_all(grad_out[chosen], 'expert', split_axis=0, concat_axis=0, t...  38.8 us
    all_to_all x1, waiting for transfers between devices, local(): lax.all_to_all(tokens[chosen], 'expert', split_axis=0, concat_axis=0, til...  34.7 us
    all_to_all x1, starting transfers between devices, local(): lax.all_to_all(gates[0], 'expert', split_axis=0, concat_axis=0, tiled=True)  16.1 us
    all_to_all x1, starting transfers between devices, local(): lax.all_to_all(gate_part.reshape(expert_count, -1), 'expert', split_axis=...  12.2 us
    psum x1, blocking collectives, local(): lax.psum(jnp.sum(total_in * (tangent_in - scaled_in * sech_in), axis=0),...  9.02 us
    all_to_all x1, waiting for transfers between devices, local(): lax.all_to_all(gates[0], 'expert', split_axis=0, concat_axis=0, tiled=True)  8.79 us
  transfers between devices with their start and end apart: 12, of which 6 were waited for; matrix products, arithmetic and copies ran while one was open for 14% of the time, Pallas kernels for 0%

commit v1 on v0

v1 whole, which is shorter than its diff:
```python
import functools

import jax
import jax.numpy as jnp
from jax import lax
from jax.experimental import pallas as pl
from jax.experimental.pallas import tpu as pltpu
from jax.sharding import PartitionSpec as P

gelu_coeff = 0.7978845608028654
cubic_coeff = 0.044715

D = 1664
HALF = 896
MIB = 1 << 20
f32, bf16 = jnp.float32, jnp.bfloat16
VMEM = pl.BlockSpec(memory_space=pltpu.VMEM)
ANY = pl.BlockSpec(memory_space=pl.ANY)
GROUPS = (0, 1, 7, 2, 6, 3, 5, 4)


def where_am_i():
    e, d, t = lax.axis_index("expert"), lax.axis_index("dp"), lax.axis_index("tensor")
    y, zl = lax.div(e, 8), lax.rem(e, 8)
    zh, c = lax.div(t, 2), lax.rem(t, 2)
    return e, d, t, y, zl, zh, c


def neighbours():
    e, d, t, y, zl, zh, c = where_am_i()
    z = zh * 8 + zl

    def at(dy, dz):
        yy, zz = lax.rem(y + dy + 4, 4), lax.rem(z + dz + 16, 16)
        return (yy * 8 + lax.rem(zz, 8), d, lax.div(zz, 8) * 2 + c)

    def along(dx):
        return (e, lax.rem(d + dx, 4), t)

    return at, along, (e, d, t + 1 - 2 * c)


def greet(devices):
    barrier = pltpu.get_barrier_semaphore()
    for device in devices:
        pl.semaphore_signal(barrier, inc=1, device_id=device, device_id_type=pl.DeviceIdType.MESH)
    pl.semaphore_wait(barrier, len(devices))


def remote(src, dst, send, recv, device):
    return pltpu.make_async_remote_copy(
        src_ref=src, dst_ref=dst, send_sem=send, recv_sem=recv,
        device_id=device, device_id_type=pl.DeviceIdType.MESH,
    )


def bring_in(
    tokens, grads, picks, gates, w_in, w_out, s_out,
    xg, win, wout, so,
    stage, local_sem, w_send, w_recv, a_send, a_recv, x_send, x_recv, f_send, f_recv, p_send, p_recv,
):
    e, d, t, y, zl, zh, c = where_am_i()
    at, along, partner = neighbours()
    greet(
        [at(dy, dz) for dz in range(-4, 5) for dy in range(4) if (dy, dz) != (0, 0)]
        + [along(dx) for dx in (1, 2, 3)]
        + [partner]
    )
    w_copies = []
    for dx in (1, 3, 2):
        there = lax.rem(d + dx, 4)
        cols = pl.ds(pl.multiple_of(there * 256, 256), 256)
        for k, (src, dst) in enumerate(
            ((w_in.at[:, cols], win.at[d]), (w_out.at[cols, :], wout.at[d]), (s_out, so.at[d]))
        ):
            copy = remote(src, dst, w_send.at[k, dx - 1], w_recv.at[k, dx - 1], along(dx))
            copy.start()
            w_copies.append(copy)
    mine = pl.ds(pl.multiple_of(d * 256, 256), 256)
    locals_ = [
        pltpu.make_async_copy(w_in.at[:, mine], win.at[d], local_sem.at[0]),
        pltpu.make_async_copy(w_out.at[mine, :], wout.at[d], local_sem.at[1]),
        pltpu.make_async_copy(s_out, so.at[d], local_sem.at[2]),
    ]
    for copy in locals_:
        copy.start()

    onehot = (lax.broadcasted_iota(jnp.int32, (256, 128), 1) == picks[...]).astype(bf16)
    body = pl.ds(pl.multiple_of(c * HALF, 128), HALF - 128)
    gate_tile = jnp.broadcast_to(gates[...], (256, 128))

    def rows(ref):
        most = jnp.dot(onehot, ref[:, body], preferred_element_type=f32)
        last = jnp.dot(onehot, ref[:, HALF - 128 : HALF], preferred_element_type=f32)
        last = jnp.where(c == 0, last, gate_tile)
        return most.reshape(32, 8, HALF - 128), last.reshape(32, 8, 128)

    x_most, x_last = rows(tokens)
    g_most, g_last = rows(grads)
    stage[:, :, 0 : HALF - 128] = jnp.concatenate([x_most, g_most], axis=1).astype(bf16)
    stage[:, :, HALF - 128 : HALF] = jnp.concatenate([x_last, g_last], axis=1).astype(bf16)

    own = pltpu.make_async_copy(stage.at[e], xg.at[0, c, 0], local_sem.at[3])
    own.start()
    for dz in GROUPS:
        for dy in range(4):
            if (dy, dz) == (0, 0):
                continue
            way = dz if dz < 4 else dz - 8
            if dz == 4:
                way = 4 if dy < 2 else -4
            device = at(dy, way)
            remote(
                stage.at[device[0]], xg.at[0, c, dz * 4 + dy], a_send.at[dz], a_recv.at[dz], device
            ).start()

    def part(block, g):
        return xg.at[block, c, pl.ds(4 * g, 4)]

    def to_partner(block, g):
        return remote(part(block, g), part(block, g), p_send.at[block, g], p_recv.at[block, g], partner)

    def forth(g):
        return remote(part(0, g), part(1, g), x_send.at[0, g], x_recv.at[0, g], along(1))

    def back(g):
        return remote(part(0, g), part(3, g), x_send.at[1, g], x_recv.at[1, g], along(3))

    def onward(g):
        if GROUPS.index(g) % 2 == 0:
            return remote(part(1, g), part(2, g), f_send.at[g], f_recv.at[g], along(1))
        return remote(part(3, g), part(2, g), f_send.at[g], f_recv.at[g], along(3))

    def arrived(g):
        n = 3 if g == 0 else 4
        ref = xg.at[0, c, pl.ds(4 * g + 4 - n, n)]
        return remote(ref, ref, a_send.at[g], a_recv.at[g], partner)

    own.wait()
    for step in range(8 + 4):
        if step < 8:
            g = GROUPS[step]
            arrived(g).wait_recv()
            forth(g).start()
            back(g).start()
            to_partner(0, g).start()
        if 2 <= step < 10:
            g = GROUPS[step - 2]
            forth(g).wait_recv()
            back(g).wait_recv()
            onward(g).start()
            to_partner(1, g).start()
            to_partner(3, g).start()
        if 4 <= step:
            g = GROUPS[step - 4]
            onward(g).wait_recv()
            to_partner(2, g).start()
    for g in GROUPS:
        arrived(g).wait_send()
        forth(g).wait_send()
        back(g).wait_send()
        onward(g).wait_send()
        for block in range(4):
            to_partner(block, g).wait()
    for copy in locals_ + w_copies:
        copy.wait()


def gelu_parts(hidden):
    inner_arg = gelu_coeff * (hidden + cubic_coeff * hidden * hidden * hidden)
    tangent = jnp.tanh(inner_arg)
    output = 0.5 * hidden * (1.0 + tangent)
    gelu_slope = 0.5 * (1.0 + tangent) + 0.5 * hidden * (1.0 - tangent * tangent) * gelu_coeff * (
        1.0 + 3.0 * cubic_coeff * hidden * hidden
    )
    return output, gelu_slope


def spread(ref, rows):
    pieces = []
    for d in range(4):
        wide = jnp.concatenate([ref[d].astype(f32), jnp.zeros((rows, 96), f32)], axis=1)
        pieces.append(pltpu.roll(wide, 32 * d, 1) if d else wide)
    out = []
    for d in range(4):
        first = pieces[d][:, :128]
        if d:
            first = first + pieces[d - 1][:, 384:]
        out += [first, pieces[d][:, 128:384]]
    out.append(pieces[3][:, 384:])
    return jnp.concatenate(out, axis=1)


def window(full, d):
    wide = full[:, 384 * d : 384 * d + 512]
    return pltpu.roll(wide, 512 - 32 * d, 1) if d else wide


def tn(a, b):
    return lax.dot_general(a, b, (((0,), (0,)), ((), ())), preferred_element_type=f32)


def nt(a, b):
    return lax.dot_general(a, b, (((1,), (1,)), ((), ())), preferred_element_type=f32)


def work(
    xg, win, wout, so, s_in, dxs, gwin, gwout, gsin, gsout,
    q_in, t_in, q_out, t_out, w_full, p_in, p_out,
):
    _, d, *_ = where_am_i()
    scale_in = s_in[:, pl.ds(pl.multiple_of(d * 256, 256), 256)]
    inv_in = 1.0 / scale_in
    for b in range(4):
        rows = slice(416 * b, 416 * b + 416)
        tangent = jnp.tanh(win[b].astype(f32) * inv_in)
        t_in[rows] = tangent
        q_in[rows] = (scale_in * tangent).astype(bf16)
    scale_out = spread(so, 1)
    inv_out = 1.0 / scale_out
    w_full[...] = spread(wout, 256)
    tangent = jnp.tanh(w_full[...] * inv_out)
    t_out[...] = tangent
    q_out[...] = (scale_out * tangent).astype(bf16)
    p_in[...] = jnp.zeros_like(p_in)
    p_out[...] = jnp.zeros_like(p_out)

    @pl.loop(0, 4)
    def _(j):
        low, high = xg[j, 0].astype(f32), xg[j, 1].astype(f32)

        def rows_of(k):
            pick = slice(8 * k, 8 * k + 8)
            left = low[:, pick].reshape(256, HALF)
            right = high[:, pick].reshape(256, HALF)
            return jnp.concatenate([left, right[:, : HALF - 128]], axis=1), right[:, HALF - 128 :]

        x, gate_tile = rows_of(0)
        g, _ = rows_of(1)
        x = x.astype(bf16)
        gate = gate_tile[:, 0:1]
        hidden = jnp.dot(x, q_in[...], preferred_element_type=f32)
        act, slope = gelu_parts(hidden)
        act = act.astype(bf16)
        back = nt(g.astype(bf16), q_out[...])
        gate_part = jnp.sum(act.astype(f32) * back, axis=1, keepdims=True)
        hidden_grad = (gate * back * slope).astype(bf16)
        out_grad = (gate * g).astype(bf16)
        p_in[...] += tn(x, hidden_grad)
        p_out[...] += tn(act, out_grad)
        dx = nt(hidden_grad, q_in[...])
        lane = lax.broadcasted_iota(jnp.int32, (256, 512), 1)
        top = gate_part.astype(bf16).astype(f32)
        rest = gate_part - top
        for k in range(4):
            piece = window(dx, k)
            piece = jnp.where(lane == 416, top, jnp.where(lane == 417, rest, piece))
            piece = piece.reshape(32, 8, 512)
            dxs[j, k % 2, k // 2] = jnp.concatenate(
                [piece[:, :, :256], piece[:, :, 256:]], axis=1
            ).astype(bf16)

    factor = 1024.0 ** -0.5
    total_s = jnp.zeros((1, 256), f32)
    for b in range(4):
        rows = slice(416 * b, 416 * b + 416)
        total = p_in[rows] * factor
        tangent = t_in[rows]
        sech = 1.0 - tangent * tangent
        gwin[b] = (total * sech).astype(bf16)
        scaled = win[b].astype(f32) * inv_in
        total_s += jnp.sum(total * (tangent - scaled * sech), axis=0, keepdims=True)
    gsin[...] = total_s
    total = p_out[...] * factor
    tangent = t_out[...]
    sech = 1.0 - tangent * tangent
    grad = total * sech
    sums = jnp.sum(total * (tangent - w_full[...] * inv_out * sech), axis=0, keepdims=True)
    for b in range(4):
        gwout[b] = window(grad, b)[:, :416].astype(bf16)
        gsout[b] = window(sums, b)


def send_out(
    dxs, gwin, gwout, gsin, gsout, picks,
    gt, gg, gw_in, gw_out, gs_in, gs_out,
    cbuf, sbuf, xbuf, rbuf, rb, obuf, tbuf, tsum,
    local_sem, c_send, c_recv, x_send, x_recv, w_send, w_recv, r_send, r_recv, t_send, t_recv,
):
    e, d, t, y, zl, zh, c = where_am_i()
    at, along, partner = neighbours()
    over, cross = at(0, 8), (e, d, 3 - t)
    greet(
        [at(dy, dz) for dz in range(16) for dy in range(4) if (dy, dz) != (0, 0)]
        + [along(dx) for dx in (1, 2, 3)]
        + [partner, cross]
    )
    c_copies = [
        remote(dxs.at[j, 1 - c], cbuf.at[j], c_send.at[j], c_recv.at[j], partner) for j in range(4)
    ]
    for j in (2, 1, 3, 0):
        c_copies[j].start()
    x_copies = []
    for j in (2, 1, 3):
        c_copies[j].wait_recv()
        for h in range(2):
            sbuf[j - 1, h] = (dxs[j, c, h].astype(f32) + cbuf[j, h].astype(f32)).astype(bf16)
        copy = remote(
            sbuf.at[j - 1], xbuf.at[j - 1], x_send.at[j - 1], x_recv.at[j - 1], along(4 - j)
        )
        copy.start()
        x_copies.append(copy)
    mine = pl.ds(pl.multiple_of(d * 256, 256), 256)
    w_copies = []
    for dx in (1, 3, 2):
        there = lax.rem(d + dx, 4)
        for k, (src, dst) in enumerate((
            (gsout.at[there], obuf.at[d]),
            (gsin, gs_in.at[d]),
            (gwin.at[there], gw_in.at[:, mine]),
            (gwout.at[there], gw_out.at[mine, :]),
        )):
            copy = remote(src, dst, w_send.at[k, dx - 1], w_recv.at[k, dx - 1], along(dx))
            copy.start()
            w_copies.append(copy)
    locals_ = [
        pltpu.make_async_copy(gsout.at[d], obuf.at[d], local_sem.at[0]),
        pltpu.make_async_copy(gsin, gs_in.at[d], local_sem.at[1]),
        pltpu.make_async_copy(gwin.at[d], gw_in.at[:, mine], local_sem.at[2]),
        pltpu.make_async_copy(gwout.at[d], gw_out.at[mine, :], local_sem.at[3]),
    ]
    for copy in locals_:
        copy.start()

    c_copies[0].wait_recv()
    for copy in x_copies:
        copy.wait_recv()
    for h in range(2):
        total = dxs[0, c, h].astype(f32) + cbuf[0, h].astype(f32)
        for k in range(3):
            total = total + xbuf[k, h].astype(f32)
        rbuf[32 * h : 32 * h + 32] = total.astype(bf16)
    own = pltpu.make_async_copy(rbuf.at[zh * 32], rb.at[zh, e], local_sem.at[4])
    own.start()
    for dz in (8, 7, 9, 6, 10, 5, 11, 4, 12, 3, 13, 2, 14, 1, 15, 0):
        for dy in range(4):
            if (dy, dz) == (0, 0):
                continue
            device = at(-dy, -dz)
            remote(
                rbuf.at[lax.div(device[2], 2) * 32 + (dz % 8) * 4 + dy], rb.at[zh, e],
                r_send, r_recv, device,
            ).start()

    locals_[0].wait()
    for copy in w_copies:
        copy.wait_recv()
    tsum[...] = obuf[0] + obuf[1] + obuf[2] + obuf[3]
    t_copies = []
    for k, device in enumerate((partner, over, cross)):
        copy = remote(tsum, tbuf.at[k], t_send.at[k], t_recv.at[k], device)
        copy.start()
        t_copies.append(copy)
    for copy in t_copies:
        copy.wait_recv()
    gs_out[...] = (tsum[...] + tbuf[0] + tbuf[1] + tbuf[2])[:, :416]

    own.wait()
    whole = rbuf.at[pl.ds(0, 63)]
    remote(whole, whole, r_send, r_recv, partner).wait()

    onehot = (lax.broadcasted_iota(jnp.int32, (256, 128), 1) == picks[...]).astype(bf16)
    left = jnp.zeros((128, 256), f32)
    right = jnp.zeros((128, 256), f32)
    gate = jnp.zeros((256, 128), f32)
    for h in range(2):
        got = rb[h].astype(f32)
        lo = got[:, :8].reshape(256, 256)
        hi = got[:, 8:].reshape(256, 256)
        left += tn(onehot, lo.astype(bf16))
        right += tn(onehot, hi.astype(bf16))
        gate += hi[:, 128:]
    gt[...] = jnp.concatenate([left, right[:, :160]], axis=1).astype(bf16)
    gg[...] = gate
    for copy in c_copies + x_copies + w_copies + t_copies:
        copy.wait_send()
    for copy in locals_[1:]:
        copy.wait()


DMA = pltpu.SemaphoreType.DMA


def struct(*shape, dtype=bf16):
    return jax.ShapeDtypeStruct(shape, dtype)


def local(tokens, grad_out, picks, gates, w_in, w_out, scale_in, scale_out):
    pick_col = picks.reshape(256, 1)
    gate_col = gates.reshape(256, 1).astype(f32)
    xg, win, wout, so = pl.pallas_call(
        bring_in,
        out_shape=(
            struct(4, 2, 32, 16, HALF),
            struct(4, 416, 256),
            struct(4, 256, 416),
            struct(4, 1, 416, dtype=f32),
        ),
        in_specs=[VMEM] * 4 + [ANY] * 2 + [VMEM],
        out_specs=(VMEM,) * 4,
        scratch_shapes=[
            pltpu.VMEM((32, 16, HALF), bf16),
            DMA((4,)),
            DMA((3, 3)), DMA((3, 3)),
            DMA((8,)), DMA((8,)),
            DMA((2, 8)), DMA((2, 8)),
            DMA((8,)), DMA((8,)),
            DMA((4, 8)), DMA((4, 8)),
        ],
        compiler_params=pltpu.CompilerParams(
            collective_id=0, has_side_effects=True, vmem_limit_bytes=40 * MIB
        ),
        name="bring_in",
    )(tokens, grad_out, pick_col, gate_col, w_in[0], w_out[0], scale_out)
    dxs, gwin, gwout, gsin, gsout = pl.pallas_call(
        work,
        out_shape=(
            struct(4, 2, 2, 32, 16, 256),
            struct(4, 416, 256),
            struct(4, 256, 416),
            struct(1, 256, dtype=f32),
            struct(4, 1, 512, dtype=f32),
        ),
        in_specs=[VMEM] * 5,
        out_specs=(VMEM,) * 5,
        scratch_shapes=[
            pltpu.VMEM((D, 256), bf16),
            pltpu.VMEM((D, 256), f32),
            pltpu.VMEM((256, D), bf16),
            pltpu.VMEM((256, D), f32),
            pltpu.VMEM((256, D), f32),
            pltpu.VMEM((D, 256), f32),
            pltpu.VMEM((256, D), f32),
        ],
        compiler_params=pltpu.CompilerParams(vmem_limit_bytes=56 * MIB),
        name="work",
    )(xg, win, wout, so, scale_in)
    gt, gg, gw_in, gw_out, gs_in, gs_out = pl.pallas_call(
        send_out,
        out_shape=(
            struct(128, 416),
            struct(256, 128, dtype=f32),
            struct(416, 1024),
            struct(1024, 416),
            struct(4, 1, 256, dtype=f32),
            struct(1, 416, dtype=f32),
        ),
        in_specs=[VMEM] * 6,
        out_specs=(VMEM, VMEM, ANY, ANY, VMEM, VMEM),
        scratch_shapes=[
            pltpu.VMEM((4, 2, 32, 16, 256), bf16),
            pltpu.VMEM((3, 2, 32, 16, 256), bf16),
            pltpu.VMEM((3, 2, 32, 16, 256), bf16),
            pltpu.VMEM((64, 16, 256), bf16),
            pltpu.VMEM((2, 32, 16, 256), bf16),
            pltpu.VMEM((4, 1, 512), f32),
            pltpu.VMEM((3, 1, 512), f32),
            pltpu.VMEM((1, 512), f32),
            DMA((5,)),
            DMA((4,)), DMA((4,)),
            DMA((3,)), DMA((3,)),
            DMA((4, 3)), DMA((4, 3)),
            DMA, DMA,
            DMA((3,)), DMA((3,)),
        ],
        compiler_params=pltpu.CompilerParams(
            collective_id=1, has_side_effects=True, vmem_limit_bytes=40 * MIB
        ),
        name="send_out",
    )(dxs, gwin, gwout, gsin, gsout, pick_col)
    gate_grad = (gg[:, 32] + gg[:, 33]).reshape(1, 32, 8)
    return gt, gate_grad, gw_in[None], gw_out[None], gs_in.reshape(1, 1024), gs_out


def solution(mesh):
    placed = (
        P(("expert", "dp"), None),
        P(("expert", "dp"), None),
        P(("expert", "dp"), None, None),
        P(("expert", "dp"), None, None),
        P("expert", "dp", "tensor"),
        P("expert", "tensor", "dp"),
        P("expert", "tensor"),
        P("expert", "dp"),
    )
    return jax.shard_map(
        local,
        mesh=mesh,
        in_specs=placed,
        out_specs=(
            P(("expert", "dp"), "tensor"),
            P(("expert", "dp"), None, None),
            P("expert", "dp", "tensor"),
            P("expert", "tensor", "dp"),
            P("expert", "tensor"),
            P("expert", "dp"),
        ),
        check_vma=False,
    )
```

time: 339 us -> 177 us (0.52)
  waiting for transfers between devices: 163 us -> 0 us
  Pallas kernels: 0 us -> 152 us
  starting transfers between devices: 51.7 us -> 0 us
  blocking collectives: 50.7 us -> 0 us
  matrix products: 21.7 us -> 0 us
  between operations: 14 us -> 0.7 us
  other arithmetic: 9.61 us -> 0.21 us
    all_to_all x7 -> x0, waiting for transfers between devices: 162 us -> none  [the longest x1 70.2 us: local(): lax.all_to_all(token_grad.reshape(expert_count, -1, feature_width), 'expe...]
    pallas_call x0 -> x3, Pallas kernels: none -> 152 us  [the longest x1 72.2 us: local(): pl.pallas_call(bring_in, out_shape=(struct(4, 2, 32, 16, HALF), struct(4,...]
    all_to_all x7 -> x0, starting transfers between devices: 51.3 us -> none  [the longest x1 16.1 us: local(): lax.all_to_all(gates[0], 'expert', split_axis=0, concat_axis=0, tiled=True)]
    psum x2 -> x0, blocking collectives: 50.7 us -> none  [the longest x1 41.7 us: local(): grad_gates = lax.psum(back_gates, 'tensor')]
    dot_general x5 -> x0, matrix products: 21.7 us -> none  [the longest x1 4.74 us: local(): lax.dot_general(picked_grad, full_out, (((1,), (1,)), ((), ())), preferre...]
    unnamed x37 -> x34, local copies, waits for them, and re-layouts: 6.84 us -> 22.2 us
    all_to_all x6 -> x0, local copies, waits for them, and re-layouts: 8.66 us -> none  [the longest x3 6.26 us: local(): lax.all_to_all(picked, 'dp', split_axis=1, concat_axis=0, tiled=True)]
    convert_element_type x3 -> x2, local copies, waits for them, and re-layouts: 6.24 us -> 0.85 us  [local(): gate_col = gates.reshape(256, 1).astype(f32)]
  transfers between devices with their start and end apart: 12 -> 0, of which waited for: 6 -> 0; matrix products, arithmetic and copies ran while one was open for 14% -> 0% of each run, Pallas kernels for 0% -> 0%
where the time goes in v1:
time: 177 us; the launch traced here: 176 us
  Pallas kernels  152 us (86%)
  local copies, waits for them, and re-layouts  23.2 us (13%)
    pallas_call x1, Pallas kernels, local(): pl.pallas_call(bring_in, out_shape=(struct(4, 2, 32, 16, HALF), struct(4,...  72.2 us
    pallas_call x1, Pallas kernels, local(): pl.pallas_call(send_out, out_shape=(struct(128, 416), struct(256, 128, dt...  64.3 us
    unnamed x34, local copies, waits for them, and re-layouts  22.2 us
    pallas_call x1, Pallas kernels, local(): pl.pallas_call(work, out_shape=(struct(4, 2, 2, 32, 16, 256), struct(4, 4...  15.5 us

profile of v1, /device:TPU:1, one launch (start us, length us, event | category | flops | bytes accessed | tf_op | source)
XLA Modules:
  0.0 176.1 jit_solution(9795515467333072888)
XLA Ops:
  0.6 0.8 copy.20
  1.4 0.8 copy.21
  2.3 1.5 copy.22
  3.8 1.1 copy-done.6
  5.0 1.0 copy-done.7
  6.0 1.0 copy-done.8
  7.0 0.7 copy-done.11
  7.7 72.2 %bring_in.1 = (bf16[4,2,32,16,896]{4,3,2,1,0:T(8,128)(2,1)S(1)}, bf16[4,416,256]{2,1,0:T(8,128)(2,1)S(1)}, bf16[4,256,416]{2,1,0:T(8,128)(2,1)S(1)}, f32[4,1,416]{2,1,0:T(1,128)S(1)}) custom-call(bf16[128,1664]{1,0:T(8,128)(2,1)S(1)} %copy-done.7, bf16[128,1664]{1,0:T(8,128)(2,1)S(1)} %copy-done.8, s32[256,1]{1,0:T(8,128)S(1)} %reshape.55.picks, ...), custom_call_target="tpu_custom_call" | custom-call | tf_op jit(solution)/shard_map/bring_in/pallas_call | solution.py:401
  79.9 2.9 %copy-done = bf16[4,2,32,16,896]{4,3,2,1,0:T(8,128)(2,1)} copy-done((bf16[4,2,32,16,896]{4,3,2,1,0:T(8,128)(2,1)}, bf16[4,2,32,16,896]{4,3,2,1,0:T(8,128)(2,1)S(1)}, u32[]{:S(2)}) %copy-start) | copy-done | bytes 7340056
  82.8 1.0 copy-done.3
  83.8 0.9 copy-done.5
  84.7 0.6 copy-done.10
  85.3 15.5 %work.1 = (bf16[4,2,2,32,16,256]{5,4,3,2,1,0:T(8,128)(2,1)}, bf16[4,416,256]{2,1,0:T(8,128)(2,1)}, bf16[4,256,416]{2,1,0:T(8,128)(2,1)}, f32[1,256]{1,0:T(1,128)}, f32[4,1,512]{2,1,0:T(1,128)}) custom-call(bf16[4,2,32,16,896]{4,3,2,1,0:T(8,128)(2,1)} %copy-done, bf16[4,416,256]{2,1,0:T(8,128)(2,1)} %copy-done.5, bf16[4,256,416]{2,1,0:T(8,128)(2,1)} %copy-done.3, ...), custom_call_target="tpu_custom_call" | custom-call | tf_op jit(solution)/shard_map/work/pallas_call | solution.py:425
  100.9 2.2 %copy-done.1 = bf16[4,2,2,32,16,256]{5,4,3,2,1,0:T(8,128)(2,1)S(1)} copy-done((bf16[4,2,2,32,16,256]{5,4,3,2,1,0:T(8,128)(2,1)S(1)}, bf16[4,2,2,32,16,256]{5,4,3,2,1,0:T(8,128)(2,1)}, u32[]{:S(2)}) %copy-start.1) | copy-done | bytes 4194328
  103.0 1.2 copy-done.2
  104.3 1.2 copy-done.4
  105.4 0.7 copy-done.9
  106.1 0.7 copy-done.12
  106.8 64.3 %send_out.1 = (bf16[128,416]{1,0:T(8,128)(2,1)S(1)}, f32[256,128]{1,0:T(8,128)S(1)}, bf16[416,1024]{1,0:T(8,128)(2,1)S(1)}, bf16[1024,416]{1,0:T(8,128)(2,1)S(1)...) custom-call(bf16[4,2,2,32,16,256]{5,4,3,2,1,0:T(8,128)(2,1)S(1)} %copy-done.1, bf16[4,416,256]{2,1,0:T(8,128)(2,1)S(1)} %copy-done.4, ...), custom_call_target="tpu_custom_call" | custom-call | tf_op jit(solution)/shard_map/send_out/pallas_call | solution.py:448
  171.1 0.8 copy.26
  172.1 0.7 copy.27
  172.8 1.2 copy.28
  174.0 0.9 copy.32
  174.9 0.6 copy.33
  (18 shorter events, 1.1 us)
Async XLA Ops:
  3.8 1.2 copy-start.6
  5.0 1.0 copy-start.7
  6.0 1.0 copy-start.8
  7.0 0.7 copy-start.11
  79.9 2.9 %copy-start = (bf16[4,2,32,16,896]{4,3,2,1,0:T(8,128)(2,1)}, bf16[4,2,32,16,896]{4,3,2,1,0:T(8,128)(2,1)S(1)}, u32[]{:S(2)}) copy-start(bf16[4,2,32,16,896]{4,3,2,1,0:T(8,128)(2,1)S(1)} %get-tuple-element.21.xg) | copy-start | bytes 22020100
  82.8 1.0 copy-start.3
  83.8 0.9 copy-start.5
  84.7 0.6 copy-start.10
  100.9 2.2 %copy-start.1 = (bf16[4,2,2,32,16,256]{5,4,3,2,1,0:T(8,128)(2,1)S(1)}, bf16[4,2,2,32,16,256]{5,4,3,2,1,0:T(8,128)(2,1)}, u32[]{:S(2)}) copy-start(bf16[4,2,2,32,16,256]{5,4,3,2,1,0:T(8,128)(2,1)} %get-tuple-element.25.dxs) | copy-start | bytes 12582916
  103.0 1.2 copy-start.2
  104.3 1.2 copy-start.4
  105.4 0.7 copy-start.9
  106.1 0.7 copy-start.12

commit v2 on v1

v2 whole, which is shorter than its diff:
```python
import functools

import jax
import jax.numpy as jnp
from jax import lax
from jax.experimental import pallas as pl
from jax.experimental.pallas import tpu as pltpu
from jax.sharding import PartitionSpec as P

gelu_coeff = 0.7978845608028654
cubic_coeff = 0.044715

D = 1664
HALF = 896
MIB = 1 << 20
f32, bf16 = jnp.float32, jnp.bfloat16
VMEM = pl.BlockSpec(memory_space=pltpu.VMEM)
ANY = pl.BlockSpec(memory_space=pl.ANY)
GROUPS = (0, 1, 7, 2, 6, 3, 5, 4)
FACTOR = 1024.0 ** -0.5


def where_am_i():
    e, d, t = lax.axis_index("expert"), lax.axis_index("dp"), lax.axis_index("tensor")
    y, zl = lax.div(e, 8), lax.rem(e, 8)
    zh, c = lax.div(t, 2), lax.rem(t, 2)
    return e, d, t, y, zl, zh, c


def neighbours():
    e, d, t, y, zl, zh, c = where_am_i()
    z = zh * 8 + zl

    def at(dy, dz):
        yy, zz = lax.rem(y + dy + 4, 4), lax.rem(z + dz + 16, 16)
        return (yy * 8 + lax.rem(zz, 8), d, lax.div(zz, 8) * 2 + c)

    def along(dx):
        return (e, lax.rem(d + dx, 4), t)

    return at, along, (e, d, t + 1 - 2 * c)


def greet(devices):
    barrier = pltpu.get_barrier_semaphore()
    for device in devices:
        pl.semaphore_signal(barrier, inc=1, device_id=device, device_id_type=pl.DeviceIdType.MESH)
    pl.semaphore_wait(barrier, len(devices))


def remote(src, dst, send, recv, device):
    return pltpu.make_async_remote_copy(
        src_ref=src, dst_ref=dst, send_sem=send, recv_sem=recv,
        device_id=device, device_id_type=pl.DeviceIdType.MESH,
    )


def gelu_parts(hidden):
    inner_arg = gelu_coeff * (hidden + cubic_coeff * hidden * hidden * hidden)
    tangent = jnp.tanh(inner_arg)
    output = 0.5 * hidden * (1.0 + tangent)
    gelu_slope = 0.5 * (1.0 + tangent) + 0.5 * hidden * (1.0 - tangent * tangent) * gelu_coeff * (
        1.0 + 3.0 * cubic_coeff * hidden * hidden
    )
    return output, gelu_slope


def window(full, d):
    wide = full[:, 384 * d : 384 * d + 512]
    return pltpu.roll(wide, 512 - 32 * d, 1) if d else wide


def tn(a, b):
    return lax.dot_general(a, b, (((0,), (0,)), ((), ())), preferred_element_type=f32)


def nt(a, b):
    return lax.dot_general(a, b, (((1,), (1,)), ((), ())), preferred_element_type=f32)


def kernel(
    tokens_hbm, grads_hbm, picks, gates, w_in, w_out, s_in, s_out,
    gt, gg, gw_in, gw_out, gs_in, gs_out,
    tokens, grads, onehot, stage, xg, win, wout, so,
    q_in, t_in, q_out, t_out, so_col, p_in, p_out,
    xs, ys, act, hid, gwin, gwout, gsin, gsout,
    dxs, cbuf, sbuf, xbuf, rbuf, rb, obuf, tbuf, tsum,
    local_sem, w_send, w_recv, a_send, a_recv, x_send, x_recv, f_send, f_recv, p_send, p_recv,
    c_send, c_recv, s_send, s_recv, g_send, g_recv, r_send, r_recv, t_send, t_recv,
):
    e, d, t, y, zl, zh, c = where_am_i()
    at, along, partner = neighbours()
    over, cross = at(0, 8), (e, d, 3 - t)
    mine = pl.ds(pl.multiple_of(d * 256, 256), 256)

    fetch = [
        pltpu.make_async_copy(tokens_hbm, tokens, local_sem.at[0]),
        pltpu.make_async_copy(grads_hbm, grads, local_sem.at[1]),
        pltpu.make_async_copy(w_in.at[:, mine], win.at[d], local_sem.at[2]),
        pltpu.make_async_copy(w_out.at[:, mine], wout.at[d], local_sem.at[3]),
        pltpu.make_async_copy(s_out, so.at[d], local_sem.at[4]),
    ]
    for copy in fetch:
        copy.start()
    greet(
        [at(dy, dz) for dz in range(16) for dy in range(4) if (dy, dz) != (0, 0)]
        + [along(dx) for dx in (1, 2, 3)]
        + [partner, cross]
    )

    w_copies = []
    for dx in (1, 3, 2):
        there = lax.rem(d + dx, 4)
        cols = pl.ds(pl.multiple_of(there * 256, 256), 256)
        for k, (src, dst) in enumerate(
            ((w_in.at[:, cols], win.at[d]), (w_out.at[:, cols], wout.at[d]), (s_out, so.at[d]))
        ):
            copy = remote(src, dst, w_send.at[k, dx - 1], w_recv.at[k, dx - 1], along(dx))
            copy.start()
            w_copies.append(copy)

    lane = lax.broadcasted_iota(jnp.int32, (8, 128), 1)
    gates32 = gates[...].astype(f32)
    onehot[...] = jnp.concatenate(
        [(lane == picks[:, k : k + 1]).astype(f32) for k in range(32)], axis=0
    ).astype(bf16)
    gate_tile = jnp.concatenate(
        [jnp.broadcast_to(gates32[:, k : k + 1], (8, 128)) for k in range(32)], axis=0
    )
    body = pl.ds(pl.multiple_of(c * HALF, 128), HALF - 128)

    def rows(ref):
        most = jnp.dot(onehot[...], ref[:, body], preferred_element_type=f32)
        last = jnp.dot(onehot[...], ref[:, HALF - 128 : HALF], preferred_element_type=f32)
        last = jnp.where(c == 0, last, gate_tile)
        return most.reshape(32, 8, HALF - 128), last.reshape(32, 8, 128)

    fetch[0].wait()
    fetch[1].wait()
    x_most, x_last = rows(tokens)
    g_most, g_last = rows(grads)
    stage[:, :, 0 : HALF - 128] = jnp.concatenate([x_most, g_most], axis=1).astype(bf16)
    stage[:, :, HALF - 128 : HALF] = jnp.concatenate([x_last, g_last], axis=1).astype(bf16)

    own = pltpu.make_async_copy(stage.at[e], xg.at[0, c, 0], local_sem.at[5])
    own.start()
    for dz in GROUPS:
        for dy in range(4):
            if (dy, dz) == (0, 0):
                continue
            way = dz if dz < 4 else dz - 8
            if dz == 4:
                way = 4 if dy < 2 else -4
            device = at(dy, way)
            remote(
                stage.at[device[0]], xg.at[0, c, dz * 4 + dy], a_send.at[dz], a_recv.at[dz], device
            ).start()

    def part(block, g):
        return xg.at[block, c, pl.ds(4 * g, 4)]

    def to_partner(block, g):
        return remote(part(block, g), part(block, g), p_send.at[block, g], p_recv.at[block, g], partner)

    def forth(g):
        return remote(part(0, g), part(1, g), x_send.at[0, g], x_recv.at[0, g], along(1))

    def back(g):
        return remote(part(0, g), part(3, g), x_send.at[1, g], x_recv.at[1, g], along(3))

    def onward(g):
        if GROUPS.index(g) % 2 == 0:
            return remote(part(1, g), part(2, g), f_send.at[g], f_recv.at[g], along(1))
        return remote(part(3, g), part(2, g), f_send.at[g], f_recv.at[g], along(3))

    def arrived(g):
        n = 3 if g == 0 else 4
        ref = xg.at[0, c, pl.ds(4 * g + 4 - n, n)]
        return remote(ref, ref, a_send.at[g], a_recv.at[g], partner)

    own.wait()
    for g in GROUPS:
        arrived(g).wait_recv()
        forth(g).start()
        back(g).start()
        to_partner(0, g).start()

    for copy in fetch[2:]:
        copy.wait()
    for copy in w_copies:
        copy.wait_recv()
    scale_in = s_in[:, mine]
    inv_in = 1.0 / scale_in
    for b in range(4):
        part_rows = slice(416 * b, 416 * b + 416)
        tangent = jnp.tanh(win[b].astype(f32) * inv_in)
        t_in[part_rows] = tangent
        q_in[part_rows] = (scale_in * tangent).astype(bf16)
        wide = jnp.concatenate([so[b], jnp.ones((1, 96), f32)], axis=1)
        col = jnp.broadcast_to(wide, (128, 512)).T[:416]
        so_col[part_rows] = col
        col = jnp.concatenate([col, col], axis=1)
        tangent = jnp.tanh(wout[b].astype(f32) * (1.0 / col))
        t_out[part_rows] = tangent
        q_out[part_rows] = (col * tangent).astype(bf16)

    c_copies = [
        remote(dxs.at[j, 1 - c], cbuf.at[j], c_send.at[j], c_recv.at[j], partner) for j in range(4)
    ]
    s_copies = [
        remote(sbuf.at[j - 1], xbuf.at[j - 1], s_send.at[j - 1], s_recv.at[j - 1], along(4 - j))
        for j in (1, 2, 3)
    ]

    def forward(j):
        for g in GROUPS:
            to_partner(j, g).wait_recv()
        low, high = xg[j, 0].astype(f32), xg[j, 1].astype(f32)

        def rows_of(k):
            pick = slice(8 * k, 8 * k + 8)
            left = low[:, pick].reshape(256, HALF)
            right = high[:, pick].reshape(256, HALF)
            return jnp.concatenate([left, right[:, : HALF - 128]], axis=1), right[:, HALF - 128 :]

        x, gate_rows = rows_of(0)
        g, _ = rows_of(1)
        x = x.astype(bf16)
        xs[j] = x
        gate = gate_rows[:, 0:1]
        ys[j] = (gate * g).astype(bf16)
        hidden = jnp.dot(x, q_in[...], preferred_element_type=f32)
        value, slope = gelu_parts(hidden)
        value = value.astype(bf16)
        act[j] = value
        back_prop = jnp.dot(g.astype(bf16), q_out[...], preferred_element_type=f32)
        gate_part = jnp.sum(value.astype(f32) * back_prop, axis=1, keepdims=True)
        hidden_grad = (gate * back_prop * slope).astype(bf16)
        hid[j] = hidden_grad
        dx = nt(hidden_grad, q_in[...])
        lanes = lax.broadcasted_iota(jnp.int32, (256, 512), 1)
        top = gate_part.astype(bf16).astype(f32)
        rest = gate_part - top
        for k in range(4):
            piece = window(dx, k)
            piece = jnp.where(lanes == 416, top, jnp.where(lanes == 417, rest, piece))
            piece = piece.reshape(32, 8, 512)
            dxs[j, k % 2, k // 2] = jnp.concatenate(
                [piece[:, :, :256], piece[:, :, 256:]], axis=1
            ).astype(bf16)
        c_copies[j].start()

    def weigh(j):
        into_in, into_out = tn(xs[j], hid[j]), tn(ys[j], act[j])
        if j:
            into_in, into_out = p_in[...] + into_in, p_out[...] + into_out
        p_in[...] = into_in
        p_out[...] = into_out

    def hand_over(j):
        c_copies[j].wait_recv()
        sbuf[j - 1] = (dxs[j, c].astype(f32) + cbuf[j].astype(f32)).astype(bf16)
        s_copies[j - 1].start()

    forward(0)
    weigh(0)
    for g in GROUPS:
        forth(g).wait_recv()
        back(g).wait_recv()
        onward(g).start()
        to_partner(1, g).start()
        to_partner(3, g).start()
    forward(1)
    weigh(1)
    hand_over(1)
    forward(3)
    for g in GROUPS:
        onward(g).wait_recv()
        to_partner(2, g).start()
    hand_over(3)
    weigh(3)
    forward(2)
    weigh(2)
    hand_over(2)

    total_s = jnp.zeros((1, 256), f32)
    for b in range(4):
        part_rows = slice(416 * b, 416 * b + 416)
        total = p_in[part_rows] * FACTOR
        tangent = t_in[part_rows]
        sech = 1.0 - tangent * tangent
        gwin[b] = (total * sech).astype(bf16)
        scaled = win[b].astype(f32) * inv_in
        total_s += jnp.sum(total * (tangent - scaled * sech), axis=0, keepdims=True)
        total = p_out[part_rows] * FACTOR
        tangent = t_out[part_rows]
        sech = 1.0 - tangent * tangent
        gwout[b] = (total * sech).astype(bf16)
        inv = 1.0 / so_col[part_rows]
        scaled = wout[b].astype(f32) * jnp.concatenate([inv, inv], axis=1)
        terms = total * (tangent - scaled * sech)
        terms = terms[:, :128] + terms[:, 128:]
        terms = jnp.concatenate([terms, jnp.zeros((96, 128), f32)], axis=0)
        gsout[b] = jnp.sum(terms.T, axis=0, keepdims=True)
    gsin[...] = total_s

    c_copies[0].wait_recv()
    total = dxs[0, c].astype(f32) + cbuf[0].astype(f32)
    for copy in s_copies:
        copy.wait_recv()
    for k in range(3):
        total = total + xbuf[k].astype(f32)
    rbuf[...] = total.astype(bf16).reshape(64, 16, 256)
    keep = pltpu.make_async_copy(rbuf.at[zh * 32], rb.at[zh, e], local_sem.at[6])
    keep.start()
    for dz in (8, 7, 9, 6, 10, 5, 11, 4, 12, 3, 13, 2, 14, 1, 15, 0):
        for dy in range(4):
            if (dy, dz) == (0, 0):
                continue
            device = at(-dy, -dz)
            remote(
                rbuf.at[lax.div(device[2], 2) * 32 + (dz % 8) * 4 + dy], rb.at[zh, e],
                r_send, r_recv, device,
            ).start()

    g_copies = []
    for k, (src, dst) in enumerate((
        (gsout, obuf.at[d]),
        (gsin, gs_in.at[d]),
        (gwin, gw_in.at[:, mine]),
        (gwout, gw_out.at[:, mine]),
    )):
        for dx in (1, 3, 2):
            block = src if k == 1 else src.at[lax.rem(d + dx, 4)]
            copy = remote(block, dst, g_send.at[k, dx - 1], g_recv.at[k, dx - 1], along(dx))
            copy.start()
            g_copies.append(copy)
    stay = [
        pltpu.make_async_copy(gsout.at[d], obuf.at[d], local_sem.at[7]),
        pltpu.make_async_copy(gsin, gs_in.at[d], local_sem.at[8]),
        pltpu.make_async_copy(gwin.at[d], gw_in.at[:, mine], local_sem.at[9]),
        pltpu.make_async_copy(gwout.at[d], gw_out.at[:, mine], local_sem.at[10]),
    ]
    for copy in stay:
        copy.start()

    stay[0].wait()
    for copy in g_copies[:3]:
        copy.wait_recv()
    tsum[...] = obuf[0] + obuf[1] + obuf[2] + obuf[3]
    t_copies = []
    for k, device in enumerate((partner, over, cross)):
        copy = remote(tsum, tbuf.at[k], t_send.at[k], t_recv.at[k], device)
        copy.start()
        t_copies.append(copy)
    for copy in t_copies:
        copy.wait_recv()
    gs_out[...] = (tsum[...] + tbuf[0] + tbuf[1] + tbuf[2])[:, :416]

    keep.wait()
    returned = rbuf.at[pl.ds(0, 63)]
    remote(returned, returned, r_send, r_recv, partner).wait()
    left = jnp.zeros((256, 128), f32)
    right = jnp.zeros((256, 128), f32)
    gate = jnp.zeros((256, 128), f32)
    for h in range(2):
        got = rb[h].astype(f32)
        lo = got[:, :8].reshape(256, 256)
        hi = got[:, 8:].reshape(256, 256)
        left += tn(lo.astype(bf16), onehot[...])
        right += tn(hi.astype(bf16), onehot[...])
        gate += hi[:, 128:]
    gt[0:256] = left.astype(bf16)
    gt[256:416] = right[:160].astype(bf16)
    gates_out = jnp.zeros((8, 128), f32)
    for k in range(32):
        rows8 = gate[8 * k : 8 * k + 8]
        gates_out = jnp.where(lane == k, rows8[:, 32:33] + rows8[:, 33:34], gates_out)
    gg[...] = gates_out[:, :32]

    for g in GROUPS:
        arrived(g).wait_send()
        forth(g).wait_send()
        back(g).wait_send()
        onward(g).wait_send()
        for block in range(4):
            to_partner(block, g).wait_send()
    for copy in w_copies + c_copies + s_copies + t_copies + g_copies:
        copy.wait_send()
    for copy in g_copies[3:]:
        copy.wait_recv()
    for copy in stay[1:]:
        copy.wait()


DMA = pltpu.SemaphoreType.DMA


def struct(*shape, dtype=bf16):
    return jax.ShapeDtypeStruct(shape, dtype)


def local(tokens, grad_out, picks, gates, w_in, w_out, scale_in, scale_out):
    gt, gg, gw_in, gw_out, gs_in, gs_out = pl.pallas_call(
        kernel,
        out_shape=(
            struct(416, 128),
            struct(8, 32, dtype=f32),
            struct(416, 1024),
            struct(416, 1024),
            struct(4, 1, 256, dtype=f32),
            struct(1, 416, dtype=f32),
        ),
        in_specs=[ANY, ANY, VMEM, VMEM, ANY, ANY, VMEM, VMEM],
        out_specs=(VMEM, VMEM, ANY, ANY, VMEM, VMEM),
        scratch_shapes=[
            pltpu.VMEM((128, D), bf16),
            pltpu.VMEM((128, D), bf16),
            pltpu.VMEM((256, 128), bf16),
            pltpu.VMEM((32, 16, HALF), bf16),
            pltpu.VMEM((4, 2, 32, 16, HALF), bf16),
            pltpu.VMEM((4, 416, 256), bf16),
            pltpu.VMEM((4, 416, 256), bf16),
            pltpu.VMEM((4, 1, 416), f32),
            pltpu.VMEM((D, 256), bf16),
            pltpu.VMEM((D, 256), f32),
            pltpu.VMEM((D, 256), bf16),
            pltpu.VMEM((D, 256), f32),
            pltpu.VMEM((D, 128), f32),
            pltpu.VMEM((D, 256), f32),
            pltpu.VMEM((D, 256), f32),
            pltpu.VMEM((4, 256, D), bf16),
            pltpu.VMEM((4, 256, D), bf16),
            pltpu.VMEM((4, 256, 256), bf16),
            pltpu.VMEM((4, 256, 256), bf16),
            pltpu.VMEM((4, 416, 256), bf16),
            pltpu.VMEM((4, 416, 256), bf16),
            pltpu.VMEM((1, 256), f32),
            pltpu.VMEM((4, 1, 512), f32),
            pltpu.VMEM((4, 2, 2, 32, 16, 256), bf16),
            pltpu.VMEM((4, 2, 32, 16, 256), bf16),
            pltpu.VMEM((3, 2, 32, 16, 256), bf16),
            pltpu.VMEM((3, 2, 32, 16, 256), bf16),
            pltpu.VMEM((64, 16, 256), bf16),
            pltpu.VMEM((2, 32, 16, 256), bf16),
            pltpu.VMEM((4, 1, 512), f32),
            pltpu.VMEM((3, 1, 512), f32),
            pltpu.VMEM((1, 512), f32),
            DMA((11,)),
            DMA((3, 3)), DMA((3, 3)),
            DMA((8,)), DMA((8,)),
            DMA((2, 8)), DMA((2, 8)),
            DMA((8,)), DMA((8,)),
            DMA((4, 8)), DMA((4, 8)),
            DMA((4,)), DMA((4,)),
            DMA((3,)), DMA((3,)),
            DMA((4, 3)), DMA((4, 3)),
            DMA, DMA,
            DMA((3,)), DMA((3,)),
        ],
        compiler_params=pltpu.CompilerParams(
            collective_id=0, has_side_effects=True, vmem_limit_bytes=58 * MIB
        ),
        name="moe_backward",
    )(
        tokens, grad_out, picks[0].T, gates[0].T, w_in[0], w_out[0].T, scale_in, scale_out,
    )
    return gt.T, gg.T[None], gw_in[None], gw_out.T[None], gs_in.reshape(1, 1024), gs_out


def solution(mesh):
    placed = (
        P(("expert", "dp"), None),
        P(("expert", "dp"), None),
        P(("expert", "dp"), None, None),
        P(("expert", "dp"), None, None),
        P("expert", "dp", "tensor"),
        P("expert", "tensor", "dp"),
        P("expert", "tensor"),
        P("expert", "dp"),
    )
    return jax.shard_map(
        local,
        mesh=mesh,
        in_specs=placed,
        out_specs=(
            P(("expert", "dp"), "tensor"),
            P(("expert", "dp"), None, None),
            P("expert", "dp", "tensor"),
            P("expert", "tensor", "dp"),
            P("expert", "tensor"),
            P("expert", "dp"),
        ),
        check_vma=False,
    )
```

time: 177 us -> 128 us (0.72)
  Pallas kernels: 152 us -> 121 us
  local copies, waits for them, and re-layouts: 23.2 us -> 6.48 us
    pallas_call x3 -> x1, Pallas kernels: 152 us -> 121 us  [local(): pl.pallas_call(kernel, out_shape=(struct(416, 128), struct(8, 32, dtype=f...]
    unnamed x34 -> x14, local copies, waits for them, and re-layouts: 22.2 us -> 6.48 us
where the time goes in v2:
time: 128 us
  Pallas kernels  121 us (95%)
  local copies, waits for them, and re-layouts  6.48 us (5%)
    pallas_call x1, Pallas kernels, local(): pl.pallas_call(kernel, out_shape=(struct(416, 128), struct(8, 32, dtype=f...  121 us
    unnamed x14, local copies, waits for them, and re-layouts  6.48 us

profile of v2, /device:TPU:1, one launch (start us, length us, event | category | flops | bytes accessed | tf_op | source)
XLA Modules:
  0.0 127.9 jit_solution(4390179534519956162)
XLA Ops:
  0.6 120.8 %moe_backward.1 = (bf16[416,128]{1,0:T(8,128)(2,1)}, f32[8,32]{1,0:T(8,128)}, bf16[416,1024]{1,0:T(8,128)(2,1)}, bf16[416,1024]{1,0:T(8,128)(2,1)}, f32[4,1,256]{2,1,0:T(1,128)}, /*index=5*/f32[1,416]{1,0:T(1,128)}) custom-call(bf16[128,1664]{1,0:T(8,128)(2,1)} %tokens_hbm.1, bf16[128,1664]{1,0:T(8,128)(2,1)} %grads_hbm.1, s32[8,32]{1,0:T(8,128)} %bitcast.24, ...), custom_call_target="tpu_custom_call" | custom-call | tf_op jit(solution)/shard_map/moe_backward/pallas_call | solution.py:404
  121.4 0.0 copy-start.2
  121.5 1.5 %copy.20 = bf16[128,416]{0,1:T(8,128)(2,1)} copy(bf16[128,416]{0,1:T(8,128)(2,1)} %bitcast.23) | data formatting | bytes 212992
  123.0 0.0 copy-done.2
  123.0 0.6 copy.21
  123.6 0.0 copy-start
  123.6 2.2 %copy.22 = bf16[1,416,1024]{2,1,0:T(8,128)(2,1)} copy(bf16[1,416,1024]{2,1,0:T(8,128)(2,1)} %bitcast.22) | data formatting | bytes 1703936
  125.8 0.0 copy-done
  125.8 0.0 copy-start.1
  125.8 0.9 copy.23
  126.7 0.0 copy-done.1
  126.7 0.0 copy-start.3
  126.7 0.6 copy.24
  127.3 0.1 copy-done.3
  127.4 0.6 copy.25
Async XLA Ops:
  121.4 1.6 %copy-start.2 = (f32[8,32]{1,0:T(8,128)S(1)}, f32[8,32]{1,0:T(8,128)}, u32[]{:S(2)}) copy-start(f32[8,32]{1,0:T(8,128)} %get-tuple-element.13) | copy-start | bytes 3076
  123.6 2.2 %copy-start = (bf16[416,1024]{1,0:T(8,128)(2,1)S(1)}, bf16[416,1024]{1,0:T(8,128)(2,1)}, u32[]{:S(2)}) copy-start(bf16[416,1024]{1,0:T(8,128)(2,1)} %get-tuple-element.15) | copy-start | bytes 2555908
  125.8 0.9 copy-start.1
  126.7 0.7 copy-start.3

commit v3 on v2

--- a/solution.py
+++ b/solution.py
@@ -45,7 +45,7 @@
     barrier = pltpu.get_barrier_semaphore()
     for device in devices:
         pl.semaphore_signal(barrier, inc=1, device_id=device, device_id_type=pl.DeviceIdType.MESH)
-    pl.semaphore_wait(barrier, len(devices))
+    return lambda: pl.semaphore_wait(barrier, len(devices))
 
 
 def remote(src, dst, send, recv, device):
@@ -84,7 +84,7 @@
     tokens, grads, onehot, stage, xg, win, wout, so,
     q_in, t_in, q_out, t_out, so_col, p_in, p_out,
     xs, ys, act, hid, gwin, gwout, gsin, gsout,
-    dxs, cbuf, sbuf, xbuf, rbuf, rb, obuf, tbuf, tsum,
+    dxs, dxg, cbuf, cgate, sbuf, sgate, vbuf, xbuf, xgate, pair, rbuf, rb, stand, obuf, tbuf, tsum,
     local_sem, w_send, w_recv, a_send, a_recv, x_send, x_recv, f_send, f_recv, p_send, p_recv,
     c_send, c_recv, s_send, s_recv, g_send, g_recv, r_send, r_recv, t_send, t_recv,
 ):
@@ -102,11 +102,36 @@
     ]
     for copy in fetch:
         copy.start()
-    greet(
-        [at(dy, dz) for dz in range(16) for dy in range(4) if (dy, dz) != (0, 0)]
-        + [along(dx) for dx in (1, 2, 3)]
+    all_in = greet(
+        [along(dx) for dx in (1, 2, 3)]
         + [partner, cross]
-    )
+        + [at(dy, dz) for dz in range(16) for dy in range(4) if (dy, dz) != (0, 0)]
+    )
+
+    lane = lax.broadcasted_iota(jnp.int32, (8, 128), 1)
+    gates32 = gates[...].astype(f32)
+    onehot[...] = jnp.concatenate(
+        [(lane == picks[:, k : k + 1]).astype(f32) for k in range(32)], axis=0
+    ).astype(bf16)
+    gate_tile = jnp.concatenate(
+        [jnp.broadcast_to(gates32[:, k : k + 1], (8, 128)) for k in range(32)], axis=0
+    )
+    body = pl.ds(pl.multiple_of(c * HALF, 128), HALF - 128)
+
+    def rows(ref):
+        most = jnp.dot(onehot[...], ref[:, body], preferred_element_type=f32)
+        last = jnp.dot(onehot[...], ref[:, HALF - 128 : HALF], preferred_element_type=f32)
+        last = jnp.where(c == 0, last, gate_tile)
+        return most.reshape(32, 8, HALF - 128), last.reshape(32, 8, 128)
+
+    fetch[0].wait()
+    fetch[1].wait()
+    x_most, x_last = rows(tokens)
+    g_most, g_last = rows(grads)
+    stage[:, :, 0 : HALF - 128] = jnp.concatenate([x_most, g_most], axis=1).astype(bf16)
+    stage[:, :, HALF - 128 : HALF] = jnp.concatenate([x_last, g_last], axis=1).astype(bf16)
+
+    all_in()
 
     w_copies = []
     for dx in (1, 3, 2):
@@ -118,29 +143,6 @@
             copy = remote(src, dst, w_send.at[k, dx - 1], w_recv.at[k, dx - 1], along(dx))
             copy.start()
             w_copies.append(copy)
-
-    lane = lax.broadcasted_iota(jnp.int32, (8, 128), 1)
-    gates32 = gates[...].astype(f32)
-    onehot[...] = jnp.concatenate(
-        [(lane == picks[:, k : k + 1]).astype(f32) for k in range(32)], axis=0
-    ).astype(bf16)
-    gate_tile = jnp.concatenate(
-        [jnp.broadcast_to(gates32[:, k : k + 1], (8, 128)) for k in range(32)], axis=0
-    )
-    body = pl.ds(pl.multiple_of(c * HALF, 128), HALF - 128)
-
-    def rows(ref):
-        most = jnp.dot(onehot[...], ref[:, body], preferred_element_type=f32)
-        last = jnp.dot(onehot[...], ref[:, HALF - 128 : HALF], preferred_element_type=f32)
-        last = jnp.where(c == 0, last, gate_tile)
-        return most.reshape(32, 8, HALF - 128), last.reshape(32, 8, 128)
-
-    fetch[0].wait()
-    fetch[1].wait()
-    x_most, x_last = rows(tokens)
-    g_most, g_last = rows(grads)
-    stage[:, :, 0 : HALF - 128] = jnp.concatenate([x_most, g_most], axis=1).astype(bf16)
-    stage[:, :, HALF - 128 : HALF] = jnp.concatenate([x_last, g_last], axis=1).astype(bf16)
 
     own = pltpu.make_async_copy(stage.at[e], xg.at[0, c, 0], local_sem.at[5])
     own.start()
@@ -205,11 +207,29 @@
         q_out[part_rows] = (col * tangent).astype(bf16)
 
     c_copies = [
-        remote(dxs.at[j, 1 - c], cbuf.at[j], c_send.at[j], c_recv.at[j], partner) for j in range(4)
-    ]
-    s_copies = [
-        remote(sbuf.at[j - 1], xbuf.at[j - 1], s_send.at[j - 1], s_recv.at[j - 1], along(4 - j))
+        (
+            remote(dxs.at[j, 1 - c], cbuf.at[j], c_send.at[0, j], c_recv.at[0, j], partner),
+            remote(dxg.at[j], cgate.at[j], c_send.at[1, j], c_recv.at[1, j], partner),
+        )
+        for j in range(4)
+    ]
+    gate_copies = [
+        remote(sgate.at[j - 1], xgate.at[j - 1], s_send.at[j - 1], s_recv.at[j - 1], along(4 - j))
         for j in (1, 2, 3)
+    ]
+    ahead = [along(1), along(3)]
+    half = [pl.ds(0, 64), pl.ds(64, 64)]
+    via = [
+        remote(sbuf.at[1, half[k]], vbuf.at[k], s_send.at[3 + k], s_recv.at[3 + k], ahead[k])
+        for k in range(2)
+    ]
+    alone = [
+        remote(sbuf.at[2 - 2 * k, half[1 - k]], xbuf.at[k, half[1 - k]], s_send.at[5 + k], s_recv.at[5 + k], ahead[k])
+        for k in range(2)
+    ]
+    joint = [
+        remote(sbuf.at[2 - 2 * k, half[k]], xbuf.at[k, half[k]], s_send.at[7 + k], s_recv.at[7 + k], ahead[k])
+        for k in range(2)
     ]
 
     def forward(j):
@@ -238,17 +258,13 @@
         hidden_grad = (gate * back_prop * slope).astype(bf16)
         hid[j] = hidden_grad
         dx = nt(hidden_grad, q_in[...])
-        lanes = lax.broadcasted_iota(jnp.int32, (256, 512), 1)
-        top = gate_part.astype(bf16).astype(f32)
-        rest = gate_part - top
-        for k in range(4):
-            piece = window(dx, k)
-            piece = jnp.where(lanes == 416, top, jnp.where(lanes == 417, rest, piece))
-            piece = piece.reshape(32, 8, 512)
-            dxs[j, k % 2, k // 2] = jnp.concatenate(
-                [piece[:, :, :256], piece[:, :, 256:]], axis=1
-            ).astype(bf16)
-        c_copies[j].start()
+        dxs[j] = dx.astype(bf16).reshape(2, 128, D)
+        compact = jnp.zeros((8, 128), f32)
+        for k in range(32):
+            compact = jnp.where(lane == k, gate_part[8 * k : 8 * k + 8], compact)
+        dxg[j] = compact
+        for copy in c_copies[j]:
+            copy.start()
 
     def weigh(j):
         into_in, into_out = tn(xs[j], hid[j]), tn(ys[j], act[j])
@@ -258,9 +274,16 @@
         p_out[...] = into_out
 
     def hand_over(j):
-        c_copies[j].wait_recv()
+        for copy in c_copies[j]:
+            copy.wait_recv()
         sbuf[j - 1] = (dxs[j, c].astype(f32) + cbuf[j].astype(f32)).astype(bf16)
-        s_copies[j - 1].start()
+        sgate[j - 1] = dxg[j] + cgate[j]
+        gate_copies[j - 1].start()
+        if j == 2:
+            for copy in via:
+                copy.start()
+        else:
+            alone[0 if j == 3 else 1].start()
 
     forward(0)
     weigh(0)
@@ -283,6 +306,13 @@
     weigh(2)
     hand_over(2)
 
+    for k in range(2):
+        via[k].wait_recv()
+        rows64 = slice(64 * k, 64 * k + 64)
+        sbuf[2 - 2 * k, rows64] = (
+            sbuf[2 - 2 * k, rows64].astype(f32) + vbuf[k].astype(f32)
+        ).astype(bf16)
+        joint[k].start()
     total_s = jnp.zeros((1, 256), f32)
     for b in range(4):
         part_rows = slice(416 * b, 416 * b + 416)
@@ -304,14 +334,36 @@
         gsout[b] = jnp.sum(terms.T, axis=0, keepdims=True)
     gsin[...] = total_s
 
-    c_copies[0].wait_recv()
-    total = dxs[0, c].astype(f32) + cbuf[0].astype(f32)
-    for copy in s_copies:
+    for copy in c_copies[0]:
         copy.wait_recv()
-    for k in range(3):
-        total = total + xbuf[k].astype(f32)
-    rbuf[...] = total.astype(bf16).reshape(64, 16, 256)
-    keep = pltpu.make_async_copy(rbuf.at[zh * 32], rb.at[zh, e], local_sem.at[6])
+    for copy in gate_copies + alone + joint:
+        copy.wait_recv()
+    total = (
+        dxs[0, c].astype(f32) + cbuf[0].astype(f32) + xbuf[0].astype(f32) + xbuf[1].astype(f32)
+    )
+    gates_sum = dxg[0] + cgate[0] + xgate[0] + xgate[1] + xgate[2]
+    gates_sum = jnp.where(c == 0, gates_sum, pltpu.roll(gates_sum, 112, 1))
+    gate_col = jnp.concatenate(
+        [jnp.broadcast_to(gates_sum[:, k : k + 1], (8, 128)) for k in range(16)], axis=0
+    )
+    top = gate_col.astype(bf16).astype(f32)
+    rest = gate_col - top
+    first = lax.broadcasted_iota(jnp.int32, (128, 128), 1)
+    extra = jnp.where(first == 32, top, rest)
+    own_half = pl.ds(pl.multiple_of(c * 16, 16), 16)
+    for k in range(4):
+        piece = window(total, k)
+        last = jnp.where((first == 32) | (first == 33), extra, piece[:, 384:])
+        piece = jnp.concatenate([piece[:, :384], last], axis=1).reshape(16, 8, 512)
+        piece = jnp.concatenate([piece[:, :, :256], piece[:, :, 256:]], axis=1).astype(bf16)
+        pair[k % 2, k // 2] = piece
+    swap = remote(
+        pair.at[1 - c], rbuf.at[:, own_half], r_send.at[1], r_recv.at[1], partner
+    )
+    swap.start()
+    rbuf[:, own_half] = pair[c]
+    swap.wait_recv()
+    keep = pltpu.make_async_copy(rbuf.at[zh, 0], rb.at[zh, e], local_sem.at[6])
     keep.start()
     for dz in (8, 7, 9, 6, 10, 5, 11, 4, 12, 3, 13, 2, 14, 1, 15, 0):
         for dy in range(4):
@@ -319,8 +371,8 @@
                 continue
             device = at(-dy, -dz)
             remote(
-                rbuf.at[lax.div(device[2], 2) * 32 + (dz % 8) * 4 + dy], rb.at[zh, e],
-                r_send, r_recv, device,
+                rbuf.at[lax.div(device[2], 2), (dz % 8) * 4 + dy], rb.at[zh, e],
+                r_send.at[0], r_recv.at[0], device,
             ).start()
 
     g_copies = []
@@ -358,8 +410,8 @@
     gs_out[...] = (tsum[...] + tbuf[0] + tbuf[1] + tbuf[2])[:, :416]
 
     keep.wait()
-    returned = rbuf.at[pl.ds(0, 63)]
-    remote(returned, returned, r_send, r_recv, partner).wait()
+    returned = stand.at[pl.ds(0, 63)]
+    remote(returned, returned, r_send.at[0], r_recv.at[0], partner).wait()
     left = jnp.zeros((256, 128), f32)
     right = jnp.zeros((256, 128), f32)
     gate = jnp.zeros((256, 128), f32)
@@ -385,8 +437,11 @@
         onward(g).wait_send()
         for block in range(4):
             to_partner(block, g).wait_send()
-    for copy in w_copies + c_copies + s_copies + t_copies + g_copies:
+    for copy in w_copies + via + alone + joint + gate_copies + t_copies + g_copies + [swap]:
         copy.wait_send()
+    for pair_of in c_copies:
+        for copy in pair_of:
+            copy.wait_send()
     for copy in g_copies[3:]:
         copy.wait_recv()
     for copy in stay[1:]:
@@ -400,17 +455,27 @@
     return jax.ShapeDtypeStruct(shape, dtype)
 
 
+def settle(*refs):
+    ins, outs, sems = refs[:6], refs[6:12], refs[12]
+    copies = [pltpu.make_async_copy(ins[k], outs[k], sems.at[k]) for k in range(6)]
+    for copy in copies:
+        copy.start()
+    for copy in copies:
+        copy.wait()
+
+
 def local(tokens, grad_out, picks, gates, w_in, w_out, scale_in, scale_out):
-    gt, gg, gw_in, gw_out, gs_in, gs_out = pl.pallas_call(
+    shapes = (
+        struct(416, 128),
+        struct(8, 32, dtype=f32),
+        struct(416, 1024),
+        struct(416, 1024),
+        struct(4, 1, 256, dtype=f32),
+        struct(1, 416, dtype=f32),
+    )
+    results = pl.pallas_call(
         kernel,
-        out_shape=(
-            struct(416, 128),
-            struct(8, 32, dtype=f32),
-            struct(416, 1024),
-            struct(416, 1024),
-            struct(4, 1, 256, dtype=f32),
-            struct(1, 416, dtype=f32),
-        ),
+        out_shape=shapes,
         in_specs=[ANY, ANY, VMEM, VMEM, ANY, ANY, VMEM, VMEM],
         out_specs=(VMEM, VMEM, ANY, ANY, VMEM, VMEM),
         scratch_shapes=[
@@ -437,12 +502,19 @@
             pltpu.VMEM((4, 416, 256), bf16),
             pltpu.VMEM((1, 256), f32),
             pltpu.VMEM((4, 1, 512), f32),
-            pltpu.VMEM((4, 2, 2, 32, 16, 256), bf16),
-            pltpu.VMEM((4, 2, 32, 16, 256), bf16),
-            pltpu.VMEM((3, 2, 32, 16, 256), bf16),
-            pltpu.VMEM((3, 2, 32, 16, 256), bf16),
+            pltpu.VMEM((4, 2, 128, D), bf16),
+            pltpu.VMEM((4, 8, 128), f32),
+            pltpu.VMEM((4, 128, D), bf16),
+            pltpu.VMEM((4, 8, 128), f32),
+            pltpu.VMEM((3, 128, D), bf16),
+            pltpu.VMEM((3, 8, 128), f32),
+            pltpu.VMEM((2, 64, D), bf16),
+            pltpu.VMEM((2, 128, D), bf16),
+            pltpu.VMEM((3, 8, 128), f32),
+            pltpu.VMEM((2, 2, 16, 16, 256), bf16),
+            pltpu.VMEM((2, 32, 16, 256), bf16),
+            pltpu.VMEM((2, 32, 16, 256), bf16),
             pltpu.VMEM((64, 16, 256), bf16),
-            pltpu.VMEM((2, 32, 16, 256), bf16),
             pltpu.VMEM((4, 1, 512), f32),
             pltpu.VMEM((3, 1, 512), f32),
             pltpu.VMEM((1, 512), f32),
@@ -452,10 +524,10 @@
             DMA((2, 8)), DMA((2, 8)),
             DMA((8,)), DMA((8,)),
             DMA((4, 8)), DMA((4, 8)),
-            DMA((4,)), DMA((4,)),
-            DMA((3,)), DMA((3,)),
+            DMA((2, 4)), DMA((2, 4)),
+            DMA((9,)), DMA((9,)),
             DMA((4, 3)), DMA((4, 3)),
-            DMA, DMA,
+            DMA((2,)), DMA((2,)),
             DMA((3,)), DMA((3,)),
         ],
         compiler_params=pltpu.CompilerParams(
@@ -465,6 +537,14 @@
     )(
         tokens, grad_out, picks[0].T, gates[0].T, w_in[0], w_out[0].T, scale_in, scale_out,
     )
+    gt, gg, gw_in, gw_out, gs_in, gs_out = pl.pallas_call(
+        settle,
+        out_shape=shapes,
+        in_specs=[ANY] * 6,
+        out_specs=(ANY,) * 6,
+        scratch_shapes=[DMA((6,))],
+        name="settle",
+    )(*results)
     return gt.T, gg.T[None], gw_in[None], gw_out.T[None], gs_in.reshape(1, 1024), gs_out
 
 

time: 128 us -> 175 us (1.37)
  Pallas kernels: 121 us -> 174 us
  local copies, waits for them, and re-layouts: 6.48 us -> 0 us
    pallas_call x1 -> x2, Pallas kernels: 121 us -> 174 us  [the longest x1 118 us: local(): pl.pallas_call(kernel, out_shape=shapes, in_specs=[ANY, ANY, VMEM, VMEM,...]
    unnamed x14 -> x0, local copies, waits for them, and re-layouts: 6.48 us -> none
where the time goes in v3:
time: 175 us
  Pallas kernels  174 us (99%)
    pallas_call x1, Pallas kernels, local(): pl.pallas_call(kernel, out_shape=shapes, in_specs=[ANY, ANY, VMEM, VMEM,...  118 us
    pallas_call x1, Pallas kernels, local(): pl.pallas_call(settle, out_shape=shapes, in_specs=[ANY] * 6, out_specs=(A...  56.3 us

profile of v3, /device:TPU:1, one launch (start us, length us, event | category | flops | bytes accessed | tf_op | source)
XLA Modules:
  0.0 174.9 jit_solution(2507565947955669760)
XLA Ops:
  0.6 117.9 %moe_backward.1 = (bf16[416,128]{1,0:T(8,128)(2,1)}, f32[8,32]{1,0:T(8,128)}, bf16[416,1024]{1,0:T(8,128)(2,1)}, bf16[416,1024]{1,0:T(8,128)(2,1)}, f32[4,1,256]{2,1,0:T(1,128)}, /*index=5*/f32[1,416]{1,0:T(1,128)}) custom-call(bf16[128,1664]{1,0:T(8,128)(2,1)} %tokens_hbm.1, bf16[128,1664]{1,0:T(8,128)(2,1)} %grads_hbm.1, s32[8,32]{1,0:T(8,128)} %bitcast.21, ...), custom_call_target="tpu_custom_call" | custom-call | tf_op jit(solution)/shard_map/moe_backward/pallas_call | solution.py:476
  118.6 56.3 %settle.1 = (bf16[416,128]{1,0:T(8,128)(2,1)}, f32[8,32]{1,0:T(8,128)}, bf16[416,1024]{1,0:T(8,128)(2,1)}, bf16[416,1024]{1,0:T(8,128)(2,1)}, f32[4,1,256]{2,1,0:T(1,128)}, /*index=5*/f32[1,416]{1,0:T(1,128)}) custom-call(bf16[416,128]{1,0:T(8,128)(2,1)} %get-tuple-element.18.refs_0_, f32[8,32]{1,0:T(8,128)} %get-tuple-element.19.refs_1_, ...), custom_call_target="tpu_custom_call" | custom-call | tf_op jit(solution)/shard_map/settle/pallas_call | solution.py:540

commit v4 on v3

--- a/solution.py
+++ b/solution.py
@@ -17,6 +17,7 @@
 VMEM = pl.BlockSpec(memory_space=pltpu.VMEM)
 ANY = pl.BlockSpec(memory_space=pl.ANY)
 GROUPS = (0, 1, 7, 2, 6, 3, 5, 4)
+HALVES = (range(0, 4), range(4, 8))
 FACTOR = 1024.0 ** -0.5
 
 
@@ -84,7 +85,7 @@
     tokens, grads, onehot, stage, xg, win, wout, so,
     q_in, t_in, q_out, t_out, so_col, p_in, p_out,
     xs, ys, act, hid, gwin, gwout, gsin, gsout,
-    dxs, dxg, cbuf, cgate, sbuf, sgate, vbuf, xbuf, xgate, pair, rbuf, rb, stand, obuf, tbuf, tsum,
+    dxs, dxg, cbuf, cgate, sbuf, sgate, vbuf, xbuf, xgate, pair, rbuf, rb, obuf, tbuf, tsum,
     local_sem, w_send, w_recv, a_send, a_recv, x_send, x_recv, f_send, f_recv, p_send, p_recv,
     c_send, c_recv, s_send, s_recv, g_send, g_recv, r_send, r_recv, t_send, t_recv,
 ):
@@ -146,7 +147,7 @@
 
     own = pltpu.make_async_copy(stage.at[e], xg.at[0, c, 0], local_sem.at[5])
     own.start()
-    for dz in GROUPS:
+    for p, dz in enumerate(GROUPS):
         for dy in range(4):
             if (dy, dz) == (0, 0):
                 continue
@@ -155,7 +156,7 @@
                 way = 4 if dy < 2 else -4
             device = at(dy, way)
             remote(
-                stage.at[device[0]], xg.at[0, c, dz * 4 + dy], a_send.at[dz], a_recv.at[dz], device
+                stage.at[device[0]], xg.at[0, c, p * 4 + dy], a_send.at[p], a_recv.at[p], device
             ).start()
 
     def part(block, g):
@@ -171,7 +172,7 @@
         return remote(part(0, g), part(3, g), x_send.at[1, g], x_recv.at[1, g], along(3))
 
     def onward(g):
-        if GROUPS.index(g) % 2 == 0:
+        if g % 2 == 0:
             return remote(part(1, g), part(2, g), f_send.at[g], f_recv.at[g], along(1))
         return remote(part(3, g), part(2, g), f_send.at[g], f_recv.at[g], along(3))
 
@@ -181,7 +182,7 @@
         return remote(ref, ref, a_send.at[g], a_recv.at[g], partner)
 
     own.wait()
-    for g in GROUPS:
+    for g in range(8):
         arrived(g).wait_recv()
         forth(g).start()
         back(g).start()
@@ -207,63 +208,73 @@
         q_out[part_rows] = (col * tangent).astype(bf16)
 
     c_copies = [
-        (
-            remote(dxs.at[j, 1 - c], cbuf.at[j], c_send.at[0, j], c_recv.at[0, j], partner),
-            remote(dxg.at[j], cgate.at[j], c_send.at[1, j], c_recv.at[1, j], partner),
-        )
-        for j in range(4)
+        [
+            (
+                remote(dxs.at[h, j, 1 - c], cbuf.at[h, j], c_send.at[0, h, j], c_recv.at[0, h, j], partner),
+                remote(dxg.at[h, j], cgate.at[h, j], c_send.at[1, h, j], c_recv.at[1, h, j], partner),
+            )
+            for j in range(4)
+        ]
+        for h in range(2)
     ]
     gate_copies = [
-        remote(sgate.at[j - 1], xgate.at[j - 1], s_send.at[j - 1], s_recv.at[j - 1], along(4 - j))
-        for j in (1, 2, 3)
+        [
+            remote(sgate.at[h, j - 1], xgate.at[h, j - 1], s_send.at[h, j - 1], s_recv.at[h, j - 1], along(4 - j))
+            for j in (1, 2, 3)
+        ]
+        for h in range(2)
     ]
     ahead = [along(1), along(3)]
-    half = [pl.ds(0, 64), pl.ds(64, 64)]
+    rows32 = [pl.ds(0, 32), pl.ds(32, 32)]
     via = [
-        remote(sbuf.at[1, half[k]], vbuf.at[k], s_send.at[3 + k], s_recv.at[3 + k], ahead[k])
-        for k in range(2)
+        [
+            remote(sbuf.at[h, 1, rows32[k]], vbuf.at[h, k], s_send.at[h, 3 + k], s_recv.at[h, 3 + k], ahead[k])
+            for k in range(2)
+        ]
+        for h in range(2)
     ]
-    alone = [
-        remote(sbuf.at[2 - 2 * k, half[1 - k]], xbuf.at[k, half[1 - k]], s_send.at[5 + k], s_recv.at[5 + k], ahead[k])
-        for k in range(2)
-    ]
-    joint = [
-        remote(sbuf.at[2 - 2 * k, half[k]], xbuf.at[k, half[k]], s_send.at[7 + k], s_recv.at[7 + k], ahead[k])
-        for k in range(2)
-    ]
-
-    def forward(j):
-        for g in GROUPS:
+
+    def to_side(h, k, rows, sem):
+        return remote(
+            sbuf.at[h, 2 - 2 * k, rows], xbuf.at[h, k, rows], s_send.at[h, sem], s_recv.at[h, sem], ahead[k]
+        )
+
+    alone = [[to_side(h, k, rows32[1 - k], 5 + k) for k in range(2)] for h in range(2)]
+    joint = [[to_side(h, k, rows32[k], 7 + k) for k in range(2)] for h in range(2)]
+
+    def forward(h, j):
+        for g in HALVES[h]:
             to_partner(j, g).wait_recv()
-        low, high = xg[j, 0].astype(f32), xg[j, 1].astype(f32)
+        blocks, at_rows = pl.ds(16 * h, 16), slice(128 * h, 128 * h + 128)
+        low, high = xg[j, 0, blocks].astype(f32), xg[j, 1, blocks].astype(f32)
 
         def rows_of(k):
             pick = slice(8 * k, 8 * k + 8)
-            left = low[:, pick].reshape(256, HALF)
-            right = high[:, pick].reshape(256, HALF)
+            left = low[:, pick].reshape(128, HALF)
+            right = high[:, pick].reshape(128, HALF)
             return jnp.concatenate([left, right[:, : HALF - 128]], axis=1), right[:, HALF - 128 :]
 
         x, gate_rows = rows_of(0)
         g, _ = rows_of(1)
         x = x.astype(bf16)
-        xs[j] = x
+        xs[j, at_rows] = x
         gate = gate_rows[:, 0:1]
-        ys[j] = (gate * g).astype(bf16)
+        ys[j, at_rows] = (gate * g).astype(bf16)
         hidden = jnp.dot(x, q_in[...], preferred_element_type=f32)
         value, slope = gelu_parts(hidden)
         value = value.astype(bf16)
-        act[j] = value
+        act[j, at_rows] = value
         back_prop = jnp.dot(g.astype(bf16), q_out[...], preferred_element_type=f32)
         gate_part = jnp.sum(value.astype(f32) * back_prop, axis=1, keepdims=True)
         hidden_grad = (gate * back_prop * slope).astype(bf16)
-        hid[j] = hidden_grad
+        hid[j, at_rows] = hidden_grad
         dx = nt(hidden_grad, q_in[...])
-        dxs[j] = dx.astype(bf16).reshape(2, 128, D)
+        dxs[h, j] = dx.astype(bf16).reshape(2, 64, D)
         compact = jnp.zeros((8, 128), f32)
-        for k in range(32):
+        for k in range(16):
             compact = jnp.where(lane == k, gate_part[8 * k : 8 * k + 8], compact)
-        dxg[j] = compact
-        for copy in c_copies[j]:
+        dxg[h, j] = compact
+        for copy in c_copies[h][j]:
             copy.start()
 
     def weigh(j):
@@ -273,46 +284,116 @@
         p_in[...] = into_in
         p_out[...] = into_out
 
-    def hand_over(j):
-        for copy in c_copies[j]:
+    def hand_over(h, j):
+        for copy in c_copies[h][j]:
             copy.wait_recv()
-        sbuf[j - 1] = (dxs[j, c].astype(f32) + cbuf[j].astype(f32)).astype(bf16)
-        sgate[j - 1] = dxg[j] + cgate[j]
-        gate_copies[j - 1].start()
+        sbuf[h, j - 1] = (dxs[h, j, c].astype(f32) + cbuf[h, j].astype(f32)).astype(bf16)
+        sgate[h, j - 1] = dxg[h, j] + cgate[h, j]
+        gate_copies[h][j - 1].start()
         if j == 2:
-            for copy in via:
+            for copy in via[h]:
                 copy.start()
         else:
-            alone[0 if j == 3 else 1].start()
-
-    forward(0)
+            alone[h][0 if j == 3 else 1].start()
+
+    def join(h):
+        for k in range(2):
+            via[h][k].wait_recv()
+            rows = slice(32 * k, 32 * k + 32)
+            sbuf[h, 2 - 2 * k, rows] = (
+                sbuf[h, 2 - 2 * k, rows].astype(f32) + vbuf[h, k].astype(f32)
+            ).astype(bf16)
+            joint[h][k].start()
+
+    def give_back(h):
+        for copy in c_copies[h][0]:
+            copy.wait_recv()
+        for copy in gate_copies[h] + alone[h] + joint[h]:
+            copy.wait_recv()
+        total = (
+            dxs[h, 0, c].astype(f32)
+            + cbuf[h, 0].astype(f32)
+            + xbuf[h, 0].astype(f32)
+            + xbuf[h, 1].astype(f32)
+        )
+        gates_sum = dxg[h, 0] + cgate[h, 0] + xgate[h, 0] + xgate[h, 1] + xgate[h, 2]
+        gates_sum = jnp.where(c == 0, gates_sum, pltpu.roll(gates_sum, 120, 1))
+        gate_col = jnp.concatenate(
+            [jnp.broadcast_to(gates_sum[:, k : k + 1], (8, 128)) for k in range(8)], axis=0
+        )
+        top = gate_col.astype(bf16).astype(f32)
+        rest = gate_col - top
+        first = lax.broadcasted_iota(jnp.int32, (64, 128), 1)
+        extra = jnp.where(first == 32, top, rest)
+        own_blocks = pl.ds(pl.multiple_of(16 * h + c * 8, 8), 8)
+        for k in range(4):
+            piece = window(total, k)
+            last = jnp.where((first == 32) | (first == 33), extra, piece[:, 384:])
+            piece = jnp.concatenate([piece[:, :384], last], axis=1).reshape(8, 8, 512)
+            piece = jnp.concatenate([piece[:, :, :256], piece[:, :, 256:]], axis=1).astype(bf16)
+            pair[h, k % 2, k // 2] = piece
+        swap = remote(
+            pair.at[h, 1 - c], rbuf.at[:, own_blocks], r_send.at[2 + h], r_recv.at[2 + h], partner
+        )
+        swap.start()
+        rbuf[:, own_blocks] = pair[h, c]
+        swap.wait_recv()
+        if h == 0:
+            keep.start()
+        for p in HALVES[h]:
+            for over_z in (8, 0):
+                for dy in range(4):
+                    dz = GROUPS[p] + over_z
+                    if (dy, dz) == (0, 0):
+                        continue
+                    device = at(-dy, -dz)
+                    remote(
+                        rbuf.at[lax.div(device[2], 2), p * 4 + dy], rb.at[zh, e],
+                        r_send.at[h], r_recv.at[h], device,
+                    ).start()
+        return swap
+
+    keep = pltpu.make_async_copy(rbuf.at[zh, 0], rb.at[zh, e], local_sem.at[6])
+
+    def pass_on(h):
+        for g in HALVES[h]:
+            forth(g).wait_recv()
+            back(g).wait_recv()
+            onward(g).start()
+            to_partner(1, g).start()
+            to_partner(3, g).start()
+
+    def last_block(h):
+        for g in HALVES[h]:
+            onward(g).wait_recv()
+            to_partner(2, g).start()
+
+    forward(0, 0)
+    forward(1, 0)
+    pass_on(0)
     weigh(0)
-    for g in GROUPS:
-        forth(g).wait_recv()
-        back(g).wait_recv()
-        onward(g).start()
-        to_partner(1, g).start()
-        to_partner(3, g).start()
-    forward(1)
+    forward(0, 1)
+    forward(0, 3)
+    hand_over(0, 1)
+    pass_on(1)
+    hand_over(0, 3)
+    last_block(0)
+    forward(1, 1)
     weigh(1)
-    hand_over(1)
-    forward(3)
-    for g in GROUPS:
-        onward(g).wait_recv()
-        to_partner(2, g).start()
-    hand_over(3)
+    forward(0, 2)
+    forward(1, 3)
+    hand_over(0, 2)
+    hand_over(1, 1)
     weigh(3)
-    forward(2)
+    hand_over(1, 3)
+    last_block(1)
+    join(0)
+    forward(1, 2)
+    swaps = [give_back(0)]
+    hand_over(1, 2)
     weigh(2)
-    hand_over(2)
-
-    for k in range(2):
-        via[k].wait_recv()
-        rows64 = slice(64 * k, 64 * k + 64)
-        sbuf[2 - 2 * k, rows64] = (
-            sbuf[2 - 2 * k, rows64].astype(f32) + vbuf[k].astype(f32)
-        ).astype(bf16)
-        joint[k].start()
+    join(1)
+
     total_s = jnp.zeros((1, 256), f32)
     for b in range(4):
         part_rows = slice(416 * b, 416 * b + 416)
@@ -334,47 +415,6 @@
         gsout[b] = jnp.sum(terms.T, axis=0, keepdims=True)
     gsin[...] = total_s
 
-    for copy in c_copies[0]:
-        copy.wait_recv()
-    for copy in gate_copies + alone + joint:
-        copy.wait_recv()
-    total = (
-        dxs[0, c].astype(f32) + cbuf[0].astype(f32) + xbuf[0].astype(f32) + xbuf[1].astype(f32)
-    )
-    gates_sum = dxg[0] + cgate[0] + xgate[0] + xgate[1] + xgate[2]
-    gates_sum = jnp.where(c == 0, gates_sum, pltpu.roll(gates_sum, 112, 1))
-    gate_col = jnp.concatenate(
-        [jnp.broadcast_to(gates_sum[:, k : k + 1], (8, 128)) for k in range(16)], axis=0
-    )
-    top = gate_col.astype(bf16).astype(f32)
-    rest = gate_col - top
-    first = lax.broadcasted_iota(jnp.int32, (128, 128), 1)
-    extra = jnp.where(first == 32, top, rest)
-    own_half = pl.ds(pl.multiple_of(c * 16, 16), 16)
-    for k in range(4):
-        piece = window(total, k)
-        last = jnp.where((first == 32) | (first == 33), extra, piece[:, 384:])
-        piece = jnp.concatenate([piece[:, :384], last], axis=1).reshape(16, 8, 512)
-        piece = jnp.concatenate([piece[:, :, :256], piece[:, :, 256:]], axis=1).astype(bf16)
-        pair[k % 2, k // 2] = piece
-    swap = remote(
-        pair.at[1 - c], rbuf.at[:, own_half], r_send.at[1], r_recv.at[1], partner
-    )
-    swap.start()
-    rbuf[:, own_half] = pair[c]
-    swap.wait_recv()
-    keep = pltpu.make_async_copy(rbuf.at[zh, 0], rb.at[zh, e], local_sem.at[6])
-    keep.start()
-    for dz in (8, 7, 9, 6, 10, 5, 11, 4, 12, 3, 13, 2, 14, 1, 15, 0):
-        for dy in range(4):
-            if (dy, dz) == (0, 0):
-                continue
-            device = at(-dy, -dz)
-            remote(
-                rbuf.at[lax.div(device[2], 2), (dz % 8) * 4 + dy], rb.at[zh, e],
-                r_send.at[0], r_recv.at[0], device,
-            ).start()
-
     g_copies = []
     for k, (src, dst) in enumerate((
         (gsout, obuf.at[d]),
@@ -396,6 +436,8 @@
     for copy in stay:
         copy.start()
 
+    swaps.append(give_back(1))
+
     stay[0].wait()
     for copy in g_copies[:3]:
         copy.wait_recv()
@@ -410,8 +452,9 @@
     gs_out[...] = (tsum[...] + tbuf[0] + tbuf[1] + tbuf[2])[:, :416]
 
     keep.wait()
-    returned = stand.at[pl.ds(0, 63)]
-    remote(returned, returned, r_send.at[0], r_recv.at[0], partner).wait()
+    for h, count in ((0, 31), (1, 32)):
+        returned = rbuf.at[0, pl.ds(0, count)]
+        remote(returned, returned, r_send.at[h], r_recv.at[h], partner).wait()
     left = jnp.zeros((256, 128), f32)
     right = jnp.zeros((256, 128), f32)
     gate = jnp.zeros((256, 128), f32)
@@ -430,18 +473,21 @@
         gates_out = jnp.where(lane == k, rows8[:, 32:33] + rows8[:, 33:34], gates_out)
     gg[...] = gates_out[:, :32]
 
-    for g in GROUPS:
+    for g in range(8):
         arrived(g).wait_send()
         forth(g).wait_send()
         back(g).wait_send()
         onward(g).wait_send()
         for block in range(4):
             to_partner(block, g).wait_send()
-    for copy in w_copies + via + alone + joint + gate_copies + t_copies + g_copies + [swap]:
+    for copy in w_copies + t_copies + g_copies + swaps:
         copy.wait_send()
-    for pair_of in c_copies:
-        for copy in pair_of:
+    for h in range(2):
+        for copy in via[h] + alone[h] + joint[h] + gate_copies[h]:
             copy.wait_send()
+        for pair_of in c_copies[h]:
+            for copy in pair_of:
+                copy.wait_send()
     for copy in g_copies[3:]:
         copy.wait_recv()
     for copy in stay[1:]:
@@ -456,11 +502,15 @@
 
 
 def settle(*refs):
-    ins, outs, sems = refs[:6], refs[6:12], refs[12]
-    copies = [pltpu.make_async_copy(ins[k], outs[k], sems.at[k]) for k in range(6)]
-    for copy in copies:
+    ins, outs, held, sems = refs[:6], refs[6:12], refs[12:18], refs[18]
+    first = [pltpu.make_async_copy(ins[k], held[k], sems.at[0, k]) for k in range(6)]
+    then = [pltpu.make_async_copy(held[k], outs[k], sems.at[1, k]) for k in range(6)]
+    for copy in first:
         copy.start()
-    for copy in copies:
+    for k in range(6):
+        first[k].wait()
+        then[k].start()
+    for copy in then:
         copy.wait()
 
 
@@ -502,19 +552,18 @@
             pltpu.VMEM((4, 416, 256), bf16),
             pltpu.VMEM((1, 256), f32),
             pltpu.VMEM((4, 1, 512), f32),
-            pltpu.VMEM((4, 2, 128, D), bf16),
-            pltpu.VMEM((4, 8, 128), f32),
-            pltpu.VMEM((4, 128, D), bf16),
-            pltpu.VMEM((4, 8, 128), f32),
-            pltpu.VMEM((3, 128, D), bf16),
-            pltpu.VMEM((3, 8, 128), f32),
-            pltpu.VMEM((2, 64, D), bf16),
-            pltpu.VMEM((2, 128, D), bf16),
-            pltpu.VMEM((3, 8, 128), f32),
-            pltpu.VMEM((2, 2, 16, 16, 256), bf16),
+            pltpu.VMEM((2, 4, 2, 64, D), bf16),
+            pltpu.VMEM((2, 4, 8, 128), f32),
+            pltpu.VMEM((2, 4, 64, D), bf16),
+            pltpu.VMEM((2, 4, 8, 128), f32),
+            pltpu.VMEM((2, 3, 64, D), bf16),
+            pltpu.VMEM((2, 3, 8, 128), f32),
+            pltpu.VMEM((2, 2, 32, D), bf16),
+            pltpu.VMEM((2, 2, 64, D), bf16),
+            pltpu.VMEM((2, 3, 8, 128), f32),
+            pltpu.VMEM((2, 2, 2, 8, 16, 256), bf16),
             pltpu.VMEM((2, 32, 16, 256), bf16),
             pltpu.VMEM((2, 32, 16, 256), bf16),
-            pltpu.VMEM((64, 16, 256), bf16),
             pltpu.VMEM((4, 1, 512), f32),
             pltpu.VMEM((3, 1, 512), f32),
             pltpu.VMEM((1, 512), f32),
@@ -524,10 +573,10 @@
             DMA((2, 8)), DMA((2, 8)),
             DMA((8,)), DMA((8,)),
             DMA((4, 8)), DMA((4, 8)),
-            DMA((2, 4)), DMA((2, 4)),
-            DMA((9,)), DMA((9,)),
+            DMA((2, 2, 4)), DMA((2, 2, 4)),
+            DMA((2, 9)), DMA((2, 9)),
             DMA((4, 3)), DMA((4, 3)),
-            DMA((2,)), DMA((2,)),
+            DMA((4,)), DMA((4,)),
             DMA((3,)), DMA((3,)),
         ],
         compiler_params=pltpu.CompilerParams(
@@ -542,7 +591,7 @@
         out_shape=shapes,
         in_specs=[ANY] * 6,
         out_specs=(ANY,) * 6,
-        scratch_shapes=[DMA((6,))],
+        scratch_shapes=[pltpu.VMEM(o.shape, o.dtype) for o in shapes] + [DMA((2, 6))],
         name="settle",
     )(*results)
     return gt.T, gg.T[None], gw_in[None], gw_out.T[None], gs_in.reshape(1, 1024), gs_out

time: 175 us -> 115 us (0.66)
  Pallas kernels: 174 us -> 114 us
    pallas_call x1, Pallas kernels: 56.3 us -> 2.52 us  [local(): pl.pallas_call(settle, out_shape=shapes, in_specs=[ANY] * 6, out_specs=(A...]
    pallas_call x1, Pallas kernels: 118 us -> 112 us  [local(): pl.pallas_call(kernel, out_shape=shapes, in_specs=[ANY, ANY, VMEM, VMEM,...]
where the time goes in v4:
time: 115 us
  Pallas kernels  114 us (99%)
    pallas_call x1, Pallas kernels, local(): pl.pallas_call(kernel, out_shape=shapes, in_specs=[ANY, ANY, VMEM, VMEM,...  112 us
    pallas_call x1, Pallas kernels, local(): pl.pallas_call(settle, out_shape=shapes, in_specs=[ANY] * 6, out_specs=(A...  2.52 us

profile of v4, /device:TPU:1, one launch (start us, length us, event | category | flops | bytes accessed | tf_op | source)
XLA Modules:
  0.0 115.2 jit_solution(6954727570226095490)
XLA Ops:
  0.6 111.9 %moe_backward.1 = (bf16[416,128]{1,0:T(8,128)(2,1)}, f32[8,32]{1,0:T(8,128)}, bf16[416,1024]{1,0:T(8,128)(2,1)}, bf16[416,1024]{1,0:T(8,128)(2,1)}, f32[4,1,256]{2,1,0:T(1,128)}, /*index=5*/f32[1,416]{1,0:T(1,128)}) custom-call(bf16[128,1664]{1,0:T(8,128)(2,1)} %tokens_hbm.1, bf16[128,1664]{1,0:T(8,128)(2,1)} %grads_hbm.1, s32[8,32]{1,0:T(8,128)} %bitcast.21, ...), custom_call_target="tpu_custom_call" | custom-call | tf_op jit(solution)/shard_map/moe_backward/pallas_call | solution.py:526
  112.5 2.5 %settle.1 = (bf16[416,128]{1,0:T(8,128)(2,1)}, f32[8,32]{1,0:T(8,128)}, bf16[416,1024]{1,0:T(8,128)(2,1)}, bf16[416,1024]{1,0:T(8,128)(2,1)}, f32[4,1,256]{2,1,0:T(1,128)}, /*index=5*/f32[1,416]{1,0:T(1,128)}) custom-call(bf16[416,128]{1,0:T(8,128)(2,1)} %get-tuple-element.18.refs_0_, f32[8,32]{1,0:T(8,128)} %get-tuple-element.19.refs_1_, ...), custom_call_target="tpu_custom_call" | custom-call | tf_op jit(solution)/shard_map/settle/pallas_call | solution.py:589

commit v5 on v4

--- a/solution.py
+++ b/solution.py
@@ -82,7 +82,7 @@
 def kernel(
     tokens_hbm, grads_hbm, picks, gates, w_in, w_out, s_in, s_out,
     gt, gg, gw_in, gw_out, gs_in, gs_out,
-    tokens, grads, onehot, stage, xg, win, wout, so,
+    tokens, grads, onehot, stage_0, stage_1, xg_0, xg_1, win, wout, so,
     q_in, t_in, q_out, t_out, so_col, p_in, p_out,
     xs, ys, act, hid, gwin, gwout, gsin, gsout,
     dxs, dxg, cbuf, cgate, sbuf, sgate, vbuf, xbuf, xgate, pair, rbuf, rb, obuf, tbuf, tsum,
@@ -93,6 +93,12 @@
     at, along, partner = neighbours()
     over, cross = at(0, 8), (e, d, 3 - t)
     mine = pl.ds(pl.multiple_of(d * 256, 256), 256)
+    stage, xg = (stage_0, stage_1), (xg_0, xg_1)
+    columns = (slice(0, HALF), slice(HALF, D))
+
+    def by_core(step):
+        for q in range(2):
+            pl.when(c == q)(functools.partial(step, q))
 
     fetch = [
         pltpu.make_async_copy(tokens_hbm, tokens, local_sem.at[0]),
@@ -114,24 +120,18 @@
     onehot[...] = jnp.concatenate(
         [(lane == picks[:, k : k + 1]).astype(f32) for k in range(32)], axis=0
     ).astype(bf16)
-    gate_tile = jnp.concatenate(
-        [jnp.broadcast_to(gates32[:, k : k + 1], (8, 128)) for k in range(32)], axis=0
-    )
-    body = pl.ds(pl.multiple_of(c * HALF, 128), HALF - 128)
-
-    def rows(ref):
-        most = jnp.dot(onehot[...], ref[:, body], preferred_element_type=f32)
-        last = jnp.dot(onehot[...], ref[:, HALF - 128 : HALF], preferred_element_type=f32)
-        last = jnp.where(c == 0, last, gate_tile)
-        return most.reshape(32, 8, HALF - 128), last.reshape(32, 8, 128)
-
+    gate_col = jnp.concatenate([gates32[:, k : k + 1] for k in range(32)], axis=0)
     fetch[0].wait()
     fetch[1].wait()
-    x_most, x_last = rows(tokens)
-    g_most, g_last = rows(grads)
-    stage[:, :, 0 : HALF - 128] = jnp.concatenate([x_most, g_most], axis=1).astype(bf16)
-    stage[:, :, HALF - 128 : HALF] = jnp.concatenate([x_last, g_last], axis=1).astype(bf16)
-
+
+    def gather(q):
+        x = jnp.dot(onehot[...], tokens[:, columns[q]], preferred_element_type=f32)
+        g = jnp.dot(onehot[...], grads[:, columns[q]], preferred_element_type=f32)
+        width = x.shape[1]
+        rows = [x.reshape(32, 8, width), (gate_col * g).reshape(32, 8, width)]
+        stage[q][...] = jnp.concatenate(rows, axis=1).astype(bf16)
+
+    by_core(gather)
     all_in()
 
     w_copies = []
@@ -145,48 +145,58 @@
             copy.start()
             w_copies.append(copy)
 
-    own = pltpu.make_async_copy(stage.at[e], xg.at[0, c, 0], local_sem.at[5])
-    own.start()
-    for p, dz in enumerate(GROUPS):
-        for dy in range(4):
-            if (dy, dz) == (0, 0):
-                continue
-            way = dz if dz < 4 else dz - 8
-            if dz == 4:
-                way = 4 if dy < 2 else -4
-            device = at(dy, way)
-            remote(
-                stage.at[device[0]], xg.at[0, c, p * 4 + dy], a_send.at[p], a_recv.at[p], device
-            ).start()
-
-    def part(block, g):
-        return xg.at[block, c, pl.ds(4 * g, 4)]
-
-    def to_partner(block, g):
-        return remote(part(block, g), part(block, g), p_send.at[block, g], p_recv.at[block, g], partner)
-
-    def forth(g):
-        return remote(part(0, g), part(1, g), x_send.at[0, g], x_recv.at[0, g], along(1))
-
-    def back(g):
-        return remote(part(0, g), part(3, g), x_send.at[1, g], x_recv.at[1, g], along(3))
-
-    def onward(g):
+    def own(q):
+        return pltpu.make_async_copy(stage[q].at[e], xg[q].at[0, 0], local_sem.at[5])
+
+    def dispatch(q):
+        own(q).start()
+        for p, dz in enumerate(GROUPS):
+            for dy in range(4):
+                if (dy, dz) == (0, 0):
+                    continue
+                way = dz if dz < 4 else dz - 8
+                if dz == 4:
+                    way = 4 if dy < 2 else -4
+                device = at(dy, way)
+                remote(
+                    stage[q].at[device[0]], xg[q].at[0, p * 4 + dy], a_send.at[p], a_recv.at[p], device
+                ).start()
+
+    by_core(dispatch)
+
+    def part(q, block, g):
+        return xg[q].at[block, pl.ds(4 * g, 4)]
+
+    def to_partner(q, block, g):
+        ref = part(q, block, g)
+        return remote(ref, ref, p_send.at[block, g], p_recv.at[block, g], partner)
+
+    def forth(q, g):
+        return remote(part(q, 0, g), part(q, 1, g), x_send.at[0, g], x_recv.at[0, g], along(1))
+
+    def back(q, g):
+        return remote(part(q, 0, g), part(q, 3, g), x_send.at[1, g], x_recv.at[1, g], along(3))
+
+    def onward(q, g):
         if g % 2 == 0:
-            return remote(part(1, g), part(2, g), f_send.at[g], f_recv.at[g], along(1))
-        return remote(part(3, g), part(2, g), f_send.at[g], f_recv.at[g], along(3))
-
-    def arrived(g):
+            return remote(part(q, 1, g), part(q, 2, g), f_send.at[g], f_recv.at[g], along(1))
+        return remote(part(q, 3, g), part(q, 2, g), f_send.at[g], f_recv.at[g], along(3))
+
+    def arrived(q, g):
         n = 3 if g == 0 else 4
-        ref = xg.at[0, c, pl.ds(4 * g + 4 - n, n)]
+        ref = xg[q].at[0, pl.ds(4 * g + 4 - n, n)]
         return remote(ref, ref, a_send.at[g], a_recv.at[g], partner)
 
-    own.wait()
-    for g in range(8):
-        arrived(g).wait_recv()
-        forth(g).start()
-        back(g).start()
-        to_partner(0, g).start()
+    def first_blocks(q):
+        own(q).wait()
+        for g in range(8):
+            arrived(q, g).wait_recv()
+            to_partner(q, 0, g).start()
+            if g < 4:
+                forth(q, g).start()
+                back(q, g).start()
+
+    by_core(first_blocks)
 
     for copy in fetch[2:]:
         copy.wait()
@@ -243,30 +253,30 @@
     joint = [[to_side(h, k, rows32[k], 7 + k) for k in range(2)] for h in range(2)]
 
     def forward(h, j):
-        for g in HALVES[h]:
-            to_partner(j, g).wait_recv()
+        def from_partner(q):
+            for g in HALVES[h]:
+                to_partner(1 - q, j, g).wait_recv()
+
+        by_core(from_partner)
         blocks, at_rows = pl.ds(16 * h, 16), slice(128 * h, 128 * h + 128)
-        low, high = xg[j, 0, blocks].astype(f32), xg[j, 1, blocks].astype(f32)
+        low, high = xg_0[j, blocks].astype(f32), xg_1[j, blocks].astype(f32)
 
         def rows_of(k):
             pick = slice(8 * k, 8 * k + 8)
             left = low[:, pick].reshape(128, HALF)
-            right = high[:, pick].reshape(128, HALF)
-            return jnp.concatenate([left, right[:, : HALF - 128]], axis=1), right[:, HALF - 128 :]
-
-        x, gate_rows = rows_of(0)
-        g, _ = rows_of(1)
-        x = x.astype(bf16)
+            right = high[:, pick].reshape(128, D - HALF)
+            return jnp.concatenate([left, right], axis=1).astype(bf16)
+
+        x, g = rows_of(0), rows_of(1)
         xs[j, at_rows] = x
-        gate = gate_rows[:, 0:1]
-        ys[j, at_rows] = (gate * g).astype(bf16)
+        ys[j, at_rows] = g
         hidden = jnp.dot(x, q_in[...], preferred_element_type=f32)
         value, slope = gelu_parts(hidden)
         value = value.astype(bf16)
         act[j, at_rows] = value
-        back_prop = jnp.dot(g.astype(bf16), q_out[...], preferred_element_type=f32)
+        back_prop = jnp.dot(g, q_out[...], preferred_element_type=f32)
         gate_part = jnp.sum(value.astype(f32) * back_prop, axis=1, keepdims=True)
-        hidden_grad = (gate * back_prop * slope).astype(bf16)
+        hidden_grad = (back_prop * slope).astype(bf16)
         hid[j, at_rows] = hidden_grad
         dx = nt(hidden_grad, q_in[...])
         dxs[h, j] = dx.astype(bf16).reshape(2, 64, D)
@@ -356,43 +366,57 @@
     keep = pltpu.make_async_copy(rbuf.at[zh, 0], rb.at[zh, e], local_sem.at[6])
 
     def pass_on(h):
-        for g in HALVES[h]:
-            forth(g).wait_recv()
-            back(g).wait_recv()
-            onward(g).start()
-            to_partner(1, g).start()
-            to_partner(3, g).start()
+        def step(q):
+            for g in HALVES[h]:
+                forth(q, g).wait_recv()
+                back(q, g).wait_recv()
+                onward(q, g).start()
+                to_partner(q, 1, g).start()
+                to_partner(q, 3, g).start()
+
+        by_core(step)
 
     def last_block(h):
-        for g in HALVES[h]:
-            onward(g).wait_recv()
-            to_partner(2, g).start()
+        def step(q):
+            for g in HALVES[h]:
+                onward(q, g).wait_recv()
+                to_partner(q, 2, g).start()
+
+        by_core(step)
+
+    def remaining(lo, hi):
+        def step(q):
+            for g in range(lo, hi):
+                forth(q, g).start()
+                back(q, g).start()
+
+        by_core(step)
 
     forward(0, 0)
+    pass_on(0)
+    remaining(4, 8)
     forward(1, 0)
-    pass_on(0)
-    weigh(0)
     forward(0, 1)
     forward(0, 3)
     hand_over(0, 1)
-    pass_on(1)
     hand_over(0, 3)
     last_block(0)
+    forward(0, 2)
+    pass_on(1)
+    hand_over(0, 2)
     forward(1, 1)
+    forward(1, 3)
+    join(0)
+    hand_over(1, 1)
+    weigh(0)
     weigh(1)
-    forward(0, 2)
-    forward(1, 3)
-    hand_over(0, 2)
-    hand_over(1, 1)
     weigh(3)
+    last_block(1)
+    forward(1, 2)
     hand_over(1, 3)
-    last_block(1)
-    join(0)
-    forward(1, 2)
+    hand_over(1, 2)
     swaps = [give_back(0)]
-    hand_over(1, 2)
     weigh(2)
-    join(1)
 
     total_s = jnp.zeros((1, 256), f32)
     for b in range(4):
@@ -415,6 +439,8 @@
         gsout[b] = jnp.sum(terms.T, axis=0, keepdims=True)
     gsin[...] = total_s
 
+    join(1)
+
     g_copies = []
     for k, (src, dst) in enumerate((
         (gsout, obuf.at[d]),
@@ -471,15 +497,18 @@
     for k in range(32):
         rows8 = gate[8 * k : 8 * k + 8]
         gates_out = jnp.where(lane == k, rows8[:, 32:33] + rows8[:, 33:34], gates_out)
-    gg[...] = gates_out[:, :32]
-
-    for g in range(8):
-        arrived(g).wait_send()
-        forth(g).wait_send()
-        back(g).wait_send()
-        onward(g).wait_send()
-        for block in range(4):
-            to_partner(block, g).wait_send()
+    gg[...] = gates_out[:, :32] / gates32
+
+    def all_sent(q):
+        for g in range(8):
+            arrived(q, g).wait_send()
+            forth(q, g).wait_send()
+            back(q, g).wait_send()
+            onward(q, g).wait_send()
+            for block in range(4):
+                to_partner(q, block, g).wait_send()
+
+    by_core(all_sent)
     for copy in w_copies + t_copies + g_copies + swaps:
         copy.wait_send()
     for h in range(2):
@@ -533,7 +562,9 @@
             pltpu.VMEM((128, D), bf16),
             pltpu.VMEM((256, 128), bf16),
             pltpu.VMEM((32, 16, HALF), bf16),
-            pltpu.VMEM((4, 2, 32, 16, HALF), bf16),
+            pltpu.VMEM((32, 16, D - HALF), bf16),
+            pltpu.VMEM((4, 32, 16, HALF), bf16),
+            pltpu.VMEM((4, 32, 16, D - HALF), bf16),
             pltpu.VMEM((4, 416, 256), bf16),
             pltpu.VMEM((4, 416, 256), bf16),
             pltpu.VMEM((4, 1, 416), f32),

time: 115 us -> 113 us (0.983)
  Pallas kernels: 114 us -> 112 us
    pallas_call x1, Pallas kernels: 112 us -> 109 us  [local(): pl.pallas_call(kernel, out_shape=shapes, in_specs=[ANY, ANY, VMEM, VMEM,...]
where the time goes in v5:
time: 113 us
  Pallas kernels  112 us (99%)
    pallas_call x1, Pallas kernels, local(): pl.pallas_call(kernel, out_shape=shapes, in_specs=[ANY, ANY, VMEM, VMEM,...  109 us
    pallas_call x1, Pallas kernels, local(): pl.pallas_call(settle, out_shape=shapes, in_specs=[ANY] * 6, out_specs=(A...  2.52 us

profile of v5, /device:TPU:1, one launch (start us, length us, event | category | flops | bytes accessed | tf_op | source)
XLA Modules:
  0.0 112.7 jit_solution(5831272238471386520)
XLA Ops:
  0.6 109.3 %moe_backward.1 = (bf16[416,128]{1,0:T(8,128)(2,1)}, f32[8,32]{1,0:T(8,128)}, bf16[416,1024]{1,0:T(8,128)(2,1)}, bf16[416,1024]{1,0:T(8,128)(2,1)}, f32[4,1,256]{2,1,0:T(1,128)}, /*index=5*/f32[1,416]{1,0:T(1,128)}) custom-call(bf16[128,1664]{1,0:T(8,128)(2,1)} %tokens_hbm.1, bf16[128,1664]{1,0:T(8,128)(2,1)} %grads_hbm.1, s32[8,32]{1,0:T(8,128)} %bitcast.21, ...), custom_call_target="tpu_custom_call" | custom-call | tf_op jit(solution)/shard_map/moe_backward/pallas_call | solution.py:555
  110.0 2.5 %settle.1 = (bf16[416,128]{1,0:T(8,128)(2,1)}, f32[8,32]{1,0:T(8,128)}, bf16[416,1024]{1,0:T(8,128)(2,1)}, bf16[416,1024]{1,0:T(8,128)(2,1)}, f32[4,1,256]{2,1,0:T(1,128)}, /*index=5*/f32[1,416]{1,0:T(1,128)}) custom-call(bf16[416,128]{1,0:T(8,128)(2,1)} %get-tuple-element.18.refs_0_, f32[8,32]{1,0:T(8,128)} %get-tuple-element.19.refs_1_, ...), custom_call_target="tpu_custom_call" | custom-call | tf_op jit(solution)/shard_map/settle/pallas_call | solution.py:620
